TPU v7x, 32 devices: a whole 2x2x4 slice. The times are simulated.
32 devices in a mesh: sect: 4 (over x, core), tile: 8 (over z, y).
Axes of the slice: x: 2, y: 2, z: 4, core: 2. Of those that a mesh axis runs over, the one named last changes fastest.
Arguments:
- spectrum: float32 [1296, 64, 128], P('sect', 'tile'), may hold values from 0.05 to 1
- courant: float32 [36], replicated, may hold values from 0.1 to 0.45
- group_ratio: float32 [36], replicated, may hold values from 0.5 to 1
- ocean_currents: float32 [2, 16384], P(None, 'tile'), may hold values from -0.15 to 0.15
- elevation: float32 [16384], P('tile'), may hold values from -0.5 to 0.5
- sea_mask: int32 [64, 128], P('tile'), may hold values 0 or 1
- owner_tile: int32 [8192, 1], P('tile'), may hold values from 0 to 7; in each aligned block of 1024 rows (0 to 1023, 1024 to 2047, ...) at most 256 rows name the same one
- ocean_slot: int32 [8192], P('tile'), may hold values from 0 to 2047
Outputs:
- new_spectrum: float32 [1296, 64, 128], P('sect', 'tile')
- ocean_stress: float32 [3, 16384], P(None, 'tile')
Inputs may be any that keep to these rules, and one draw needn't show every extreme that they name: `owner_tile`: among the wave cells of one tile at most 256 name the same owner tile, a bound that some block reaches of them.
All inputs are finite; a program needn't handle non-finite values. No bound on the sum of `sea_mask` on one device may be relied on, other than what follows from the above.
Results may differ from a plain program's by a relative error of at most 0.00011.
Values sent between devices are 32-bit elements; how exact they have to be, the bound alone decides.
A program may use at most 64 MiB of HBM per device.

v0:
```python
import math

import jax
import jax.numpy as jnp
from jax import lax
from jax.sharding import PartitionSpec as P

NDIR = 36
NFREQ = 36
STEPS = 4


def with_halo(x, sides, width):
    for axis, dim in sides:
        size, length = (lax.axis_size(axis), x.shape[dim])
        up = [(i, (i + 1) % size) for i in range(size - 1)]
        down = [(j, i) for i, j in up]
        last = lax.slice_in_dim(x, length - width, length, axis=dim)
        leading = lax.slice_in_dim(x, 0, width, axis=dim)
        before = lax.ppermute(last, axis, up)
        after = lax.ppermute(leading, axis, down)
        x = jnp.concatenate([before, x, after], axis=dim)
    return x


def advance(energy, flow_fields, speed_x, speed_y):
    vel_x = speed_x + flow_fields[0]
    vel_y = speed_y + flow_fields[1]
    middle = energy[:, 1:-1]
    mid_vel = vel_x[:, 1:-1]
    face_x = 0.5 * (mid_vel + jnp.roll(mid_vel, -1, axis=2))
    east_side = jnp.roll(middle, -1, axis=2)
    flux_x = jnp.maximum(face_x, 0.0) * middle + jnp.minimum(face_x, 0.0) * east_side
    div_x = flux_x - jnp.roll(flux_x, 1, axis=2)
    face_y = 0.5 * (vel_y[:, :-1] + vel_y[:, 1:])
    flux_y = jnp.maximum(face_y, 0.0) * energy[:, :-1] + jnp.minimum(face_y, 0.0) * energy[:, 1:]
    div_y = flux_y[:, 1:] - flux_y[:, :-1]
    return flow_fields[2, 1:-1] * (middle - div_x - div_y)


def local(
    spectrum, courant, group_ratio, ocean_currents, elevation, sea_mask, owner_tile, ocean_slot
):
    bin_count, row_count, columns = spectrum.shape
    cell_count = row_count * columns
    tile_count = lax.axis_size("tile")
    capacity = 2 * ((cell_count + tile_count - 1) // tile_count)
    ocean_cells = elevation.shape[0]
    first_bin = lax.axis_index("sect") * bin_count
    bin_ids = first_bin + jnp.arange(bin_count, dtype=jnp.int32)
    dir_ids = bin_ids // NFREQ
    freq_ids = bin_ids % NFREQ
    freq_pick = (freq_ids[:, None] == jnp.arange(NFREQ, dtype=jnp.int32)[None, :]).astype(
        jnp.float32
    )
    group_speed = jnp.sum(freq_pick * courant[None, :], 1)
    ratio_bin = jnp.sum(freq_pick * group_ratio[None, :], 1)
    angles = (dir_ids.astype(jnp.float32) + 0.5) * (2.0 * math.pi / NDIR)
    cos_dir = jnp.cos(angles)
    sin_dir = jnp.sin(angles)
    speed_x = (group_speed * cos_dir)[:, None, None]
    speed_y = (group_speed * sin_dir)[:, None, None]
    owners = owner_tile[:, 0]
    one_hot = (owners[:, None] == jnp.arange(tile_count, dtype=jnp.int32)[None, :]).astype(
        jnp.int32
    )
    earlier = jnp.cumsum(one_hot, 0) - one_hot
    rank_in = jnp.sum(earlier * one_hot, 1)
    position = owners * capacity + rank_in
    requests = jnp.full((tile_count * capacity,), -1, jnp.int32).at[position].set(ocean_slot)
    asked_slots = lax.all_to_all(
        requests.reshape(tile_count, capacity), "tile", split_axis=0, concat_axis=0, tiled=True
    )
    is_valid = asked_slots >= 0
    slot_index = jnp.where(is_valid, asked_slots, 0)
    surface = jnp.concatenate([ocean_currents, elevation[None]], 0)
    answer = jnp.where(is_valid[None], surface[:, slot_index], 0.0)
    returned = lax.all_to_all(answer, "tile", split_axis=1, concat_axis=1, tiled=True)
    at_cells = returned.reshape(3, tile_count * capacity)[:, position]
    sea_float = sea_mask.astype(jnp.float32)
    flow_fields = jnp.concatenate([at_cells[:2].reshape(2, row_count, columns), sea_float[None]], 0)
    energy = spectrum
    for sub_step in range(STEPS):
        extended = with_halo(jnp.concatenate([energy, flow_fields], 0), (("tile", 1),), 1)
        energy = advance(extended[:bin_count], extended[bin_count:], speed_x, speed_y)
    weights = jnp.stack(
        [
            ratio_bin * (1.0 + cos_dir * cos_dir) - 0.5,
            ratio_bin * cos_dir * sin_dir,
            ratio_bin * (1.0 + sin_dir * sin_dir) - 0.5,
        ],
        0,
    ) * (4.0 / (NDIR * NFREQ))
    partial_value = jnp.dot(
        weights, energy.reshape(bin_count, cell_count), precision=lax.Precision.HIGHEST
    )
    partial_value = partial_value * ((1.0 + at_cells[2]) * sea_float.reshape(-1))
    partial_value = lax.psum(partial_value, "sect")
    packed = jnp.zeros((3, tile_count * capacity), jnp.float32).at[:, position].set(partial_value)
    arrived = lax.all_to_all(
        packed.reshape(3, tile_count, capacity), "tile", split_axis=1, concat_axis=1, tiled=True
    )
    flat_index = slot_index.reshape(-1)
    weight = is_valid.reshape(-1).astype(jnp.float32)
    totals = (
        jnp.zeros((3, ocean_cells), jnp.float32)
        .at[:, flat_index]
        .add(arrived.reshape(3, -1) * weight[None])
    )
    counts = jnp.zeros((ocean_cells,), jnp.float32).at[flat_index].add(weight)
    return (energy, totals / jnp.maximum(counts, 1.0)[None])


def solution(mesh):
    in_specs = (
        P("sect", "tile", None),
        P(),
        P(),
        P(None, "tile"),
        P("tile"),
        P("tile", None),
        P("tile", None),
        P("tile"),
    )
    out_specs = (P("sect", "tile", None), P(None, "tile"))
    return jax.shard_map(local, mesh=mesh, in_specs=in_specs, out_specs=out_specs, check_vma=False)
```

profile of v0, /device:TPU:0, one launch (start us, length us, event | category | flops | bytes accessed | tf_op | source)
XLA Modules:
  0.0 170.9 jit_solution(4553993287614038351)
XLA Ops:
  1.3 2.3 %reduce-window.6 = s32[8,8,128]{2,1,0:T(8,128)S(1)} reduce-window(s32[8,8,128]{2,1,0:T(8,128)S(1)} %fusion.61, s32[]{:T(128)} %constant.22.clone.1), window={size=1x1x128 pad=0_0x0_0x127_0}, to_apply=%region_1.2 | reduce-window | flops 1040384 | bytes 65540 | tf_op jit(solution)/shard_map/reduce-window
  5.5 5.0 %scatter_custom_fusion = s32[2048]{0:T(1024)} fusion(s32[1024]{0:T(1024)S(1)} %bitcast.105, s32[1024]{0:T(1024)} %param.15, s32[]{:T(128)} %constant.25.clone.1), kind=kCustom, calls=%fused_computation.167 | custom fusion | bytes 8704 | tf_op jit(solution)/shard_map/scatter | solution.py:70
  10.6 7.3 %all-to-all-start = ((s32[8,1,256]{2,1,0:T(1,128)}), s32[8,1,256]{2,1,0:T(1,128)S(1)}, u32[]{:S(2)}, u32[]{:S(2)}) async-start(s32[8,1,256]{2,1,0:T(1,128)} %bitcast.5), calls=%async_computation | async-start | bytes 16384 | tf_op jit(solution)/shard_map/all_to_all | solution.py:71
  19.8 4.5 %all-to-all-done = s32[8,1,256]{2,1,0:T(1,128)S(1)} async-done(((s32[8,1,256]{2,1,0:T(1,128)}), s32[8,1,256]{2,1,0:T(1,128)S(1)}, u32[]{:S(2)}, u32[]{:S(2)}) %all-to-all-start) | async-done | bytes 8224 | tf_op jit(solution)/shard_map/all_to_all | solution.py:71
  24.4 7.6 %gather_fusion = f32[2048,3]{1,0:T(8,128)} fusion(f32[3,2048]{0,1:T(8,128)S(1)} %copy.85, s32[2048]{0:T(1024)S(1)} %broadcast_clamp_fusion), kind=kCustom, calls=%fused_computation | custom fusion | bytes 57344 | tf_op jit(solution)/shard_map/gather | solution.py:77
  34.2 3.3 %all-to-all-start.1 = ((f32[3,8,256]{2,0,1:T(4,128)}), f32[3,8,256]{2,0,1:T(4,128)S(1)}, u32[]{:S(2)}, u32[]{:S(2)}) async-start(f32[3,8,256]{2,0,1:T(4,128)} %select_bitcast_fusion), calls=%async_computation.1 | async-start | bytes 65536 | tf_op jit(solution)/shard_map/all_to_all | solution.py:78
  38.1 6.1 %all-to-all-done.1 = f32[3,8,256]{2,0,1:T(4,128)S(1)} async-done(((f32[3,8,256]{2,0,1:T(4,128)}), f32[3,8,256]{2,0,1:T(4,128)S(1)}, u32[]{:S(2)}, u32[]{:S(2)}) %all-to-all-start.1) | async-done | bytes 24608 | tf_op jit(solution)/shard_map/all_to_all | solution.py:78
  45.5 4.0 %gather_fusion.1 = f32[1024,3]{1,0:T(8,128)S(1)} fusion(f32[3,2048]{0,1:T(8,128)} %bitcast.93, s32[1024]{0:T(1024)S(1)} %broadcast_clamp_fusion.1), kind=kCustom, calls=%fused_computation.1 | custom fusion | bytes 28672 | tf_op jit(solution)/shard_map/gather | solution.py:79
  51.4 4.6 %collective-permute-start = (f32[327,1,128]{2,0,1:T(8,128)S(1)}, f32[327,1,128]{2,0,1:T(8,128)S(1)}, u32[]{:S(2)}, u32[]{:S(2)}) collective-permute-start(f32[327,1,128]{2,0,1:T(8,128)S(1)} %copy.89), channel_id=1, source_target_pairs={{0,1},{1,2},{2,3},{3,4},{4,5},{5,6},{6,7},{8,9},{9,10},{10,11},{11... | collective-permute-start | bytes 502280 | tf_op jit(solution)/shard_map/ppermute | solution.py:20
  60.9 2.1 %fusion.10 = f32[324,9,128]{2,1,0:T(8,128)S(1)} fusion(f32[1,8,128]{2,1,0:T(8,128)S(1)} %get-tuple-element.33, f32[2,8,128]{2,1,0:T(8,128)S(1)} %copy.88, f32[327,1,128]{2,1,0:T(1,128)S(1)} %copy.92, f32[324,8,128]{2,1,0:T(8,128)S(1)} %copy-done, f32[327,1,128]{2,1,0:T(1,128)S(1)} %copy.91, f32[324,10,128]{2,1,0:T(8,128)S(1)} %get-tuple-element.39), kind=kLoop, calls=%fused_computation.48 | loop fusion | flops 4852224 | bytes 6153216 | tf_op jit(solution)/shard_map/add | solution.py:36
  66.7 5.2 %collective-permute-start.2 = (f32[327,1,128]{2,0,1:T(8,128)S(1)}, f32[327,1,128]{2,0,1:T(8,128)S(1)}, u32[]{:S(2)}, u32[]{:S(2)}) collective-permute-start(f32[327,1,128]{2,0,1:T(8,128)S(1)} %copy.96), channel_id=1, source_target_pairs={{0,1},{1,2},{2,3},{3,4},{4,5},{5,6},{6,7},{8,9},{9,10},{10,11},{11... | collective-permute-start | bytes 502280 | tf_op jit(solution)/shard_map/ppermute | solution.py:20
  73.2 2.3 %collective-permute-done.2 = f32[327,1,128]{2,0,1:T(8,128)S(1)} collective-permute-done((f32[327,1,128]{2,0,1:T(8,128)S(1)}, f32[327,1,128]{2,0,1:T(8,128)S(1)}, u32[]{:S(2)}, u32[]{:S(2)}) %collective-permute-start.2) | collective-permute-done | bytes 167456 | tf_op jit(solution)/shard_map/ppermute | solution.py:20
  79.1 2.0 %fusion.13 = f32[324,9,128]{2,1,0:T(8,128)S(1)} fusion(f32[1,8,128]{2,1,0:T(8,128)S(1)} %get-tuple-element.33, f32[2,8,128]{2,1,0:T(8,128)S(1)} %copy.88, f32[327,1,128]{2,1,0:T(1,128)S(1)} %copy.99, f32[324,8,128]{2,1,0:T(8,128)S(1)} %fusion.42, f32[327,1,128]{2,1,0:T(1,128)S(1)} %copy.98, f32[324,10,128]{2,1,0:T(8,128)S(1)} %broadcast_add_fusion.4), kind=kLoop, calls=%fused_computation.51 | loop fusion | flops 4852224 | bytes 6153216 | tf_op jit(solution)/shard_map/add | solution.py:36
  83.4 5.0 %collective-permute-start.4 = (f32[327,1,128]{2,0,1:T(8,128)S(1)}, f32[327,1,128]{2,0,1:T(8,128)S(1)}, u32[]{:S(2)}, u32[]{:S(2)}) collective-permute-start(f32[327,1,128]{2,0,1:T(8,128)S(1)} %copy.103), channel_id=1, source_target_pairs={{0,1},{1,2},{2,3},{3,4},{4,5},{5,6},{6,7},{8,9},{9,10},{10,11},{11... | collective-permute-start | bytes 502280 | tf_op jit(solution)/shard_map/ppermute | solution.py:20
  90.2 2.9 %collective-permute-done.4 = f32[327,1,128]{2,0,1:T(8,128)S(1)} collective-permute-done((f32[327,1,128]{2,0,1:T(8,128)S(1)}, f32[327,1,128]{2,0,1:T(8,128)S(1)}, u32[]{:S(2)}, u32[]{:S(2)}) %collective-permute-start.4) | collective-permute-done | bytes 167456 | tf_op jit(solution)/shard_map/ppermute | solution.py:20
  96.6 2.0 %fusion.16 = f32[324,9,128]{2,1,0:T(8,128)S(1)} fusion(f32[1,8,128]{2,1,0:T(8,128)S(1)} %get-tuple-element.33, f32[2,8,128]{2,1,0:T(8,128)S(1)} %copy.88, f32[327,1,128]{2,1,0:T(1,128)S(1)} %copy.106, f32[324,8,128]{2,1,0:T(8,128)S(1)} %fusion.39, f32[327,1,128]{2,1,0:T(1,128)S(1)} %copy.105, f32[324,10,128]{2,1,0:T(8,128)S(1)} %broadcast_add_fusion.2), kind=kLoop, calls=%fused_computation.54 | loop fusion | flops 4852224 | bytes 6153216 | tf_op jit(solution)/shard_map/add | solution.py:36
  101.0 5.2 %collective-permute-start.6 = (f32[327,1,128]{2,0,1:T(8,128)S(1)}, f32[327,1,128]{2,0,1:T(8,128)S(1)}, u32[]{:S(2)}, u32[]{:S(2)}) collective-permute-start(f32[327,1,128]{2,0,1:T(8,128)S(1)} %copy.110), channel_id=1, source_target_pairs={{0,1},{1,2},{2,3},{3,4},{4,5},{5,6},{6,7},{8,9},{9,10},{10,11},{11... | collective-permute-start | bytes 502280 | tf_op jit(solution)/shard_map/ppermute | solution.py:20
  106.2 13.9 %scatter_custom_fusion.3 = f32[2048]{0:T(1024)S(1)} fusion(s32[2048]{0:T(1024)S(1)} %bitcast.111, f32[2048]{0:T(1024)S(1)} %bitcast.101, f32[]{:T(128)} %constant.23.clone.1), kind=kCustom, calls=%fused_computation.165 | custom fusion | flops 2048 | bytes 8196 | tf_op jit(solution)/shard_map/scatter-add | solution.py:110
  124.6 2.1 %fusion.19 = f32[324,9,128]{2,1,0:T(8,128)S(1)} fusion(f32[1,8,128]{2,1,0:T(8,128)S(1)} %get-tuple-element.33, f32[2,8,128]{2,1,0:T(8,128)S(1)} %copy.88, f32[327,1,128]{2,1,0:T(1,128)S(1)} %copy.113, f32[324,8,128]{2,1,0:T(8,128)S(1)} %fusion.36, f32[327,1,128]{2,1,0:T(1,128)S(1)} %copy.112, f32[324,10,128]{2,1,0:T(8,128)S(1)} %broadcast_add_fusion), kind=kLoop, calls=%fused_computation.57 | loop fusion | flops 4852224 | bytes 6153216 | tf_op jit(solution)/shard_map/add | solution.py:36
  129.1 10.1 %psum.7 = f32[3,1024]{1,0:T(4,128)S(1)} all-reduce(f32[3,1024]{1,0:T(4,128)S(1)} %convolution_multiply_fusion), channel_id=1, replica_groups=mesh['sect'=4,'tile'=8] {'sect'}, use_global_device_ids=true, to_apply=%region_6.7 | all-reduce | flops 3072 | bytes 24576 | tf_op jit(solution)/shard_map/psum | solution.py:98
  139.4 3.3 %scatter_custom_fusion.1 = f32[3,2048]{0,1:T(8,128)S(1)} fusion(s32[1024]{0:T(1024)S(1)} %bitcast.107, f32[1024,3]{1,0:T(8,128)S(1)} %copy.117, f32[]{:T(128)} %constant.23.clone.1), kind=kCustom, calls=%fused_computation.125 | custom fusion | bytes 24580 | tf_op jit(solution)/shard_map/scatter | solution.py:99
  143.7 4.8 %all-to-all-start.2 = ((f32[3,8,256]{2,0,1:T(4,128)}), f32[3,8,256]{2,0,1:T(4,128)S(1)}, u32[]{:S(2)}, u32[]{:S(2)}) async-start(f32[3,8,256]{2,0,1:T(4,128)} %copy.118), calls=%async_computation.2 | async-start | bytes 65536 | tf_op jit(solution)/shard_map/all_to_all | solution.py:100
  148.5 6.7 %all-to-all-done.2 = f32[3,8,256]{2,0,1:T(4,128)S(1)} async-done(((f32[3,8,256]{2,0,1:T(4,128)}), f32[3,8,256]{2,0,1:T(4,128)S(1)}, u32[]{:S(2)}, u32[]{:S(2)}) %all-to-all-start.2) | async-done | bytes 24608 | tf_op jit(solution)/shard_map/all_to_all | solution.py:100
  155.5 14.0 %scatter_custom_fusion.2 = f32[3,2048]{0,1:T(8,128)S(1)} fusion(s32[2048]{0:T(1024)S(1)} %bitcast.112, f32[2048,3]{1,0:T(8,128)S(1)} %copy.119, f32[]{:T(128)} %constant.23.clone.1), kind=kCustom, calls=%fused_computation.123 | custom fusion | flops 6144 | bytes 24580 | tf_op jit(solution)/shard_map/scatter-add | solution.py:108
  (118 shorter events, 43.0 us)
Async XLA Ops:
  10.6 13.8 %all-to-all-start = ((s32[8,1,256]{2,1,0:T(1,128)}), s32[8,1,256]{2,1,0:T(1,128)S(1)}, u32[]{:S(2)}, u32[]{:S(2)}) async-start(s32[8,1,256]{2,1,0:T(1,128)} %bitcast.5), calls=%async_computation | async-start | bytes 16384 | tf_op jit(solution)/shard_map/all_to_all | solution.py:71
  17.8 19.7 %copy-start.3 = (f32[36]{0:T(128)S(1)}, f32[36]{0:T(128)}, u32[]{:S(2)}) copy-start(f32[36]{0:T(128)} %param.10) | copy-start | bytes 436
  17.8 19.7 %copy-start.4 = (f32[36]{0:T(128)S(1)}, f32[36]{0:T(128)}, u32[]{:S(2)}) copy-start(f32[36]{0:T(128)} %param.9) | copy-start | bytes 436
  17.9 19.8 %copy-start = (f32[324,8,128]{2,1,0:T(8,128)S(1)}, f32[324,8,128]{2,1,0:T(8,128)}, u32[]{:S(2)}) copy-start(f32[324,8,128]{2,1,0:T(8,128)} %param.8) | copy-start | bytes 3981316
  34.2 10.0 %all-to-all-start.1 = ((f32[3,8,256]{2,0,1:T(4,128)}), f32[3,8,256]{2,0,1:T(4,128)S(1)}, u32[]{:S(2)}, u32[]{:S(2)}) async-start(f32[3,8,256]{2,0,1:T(4,128)} %select_bitcast_fusion), calls=%async_computation.1 | async-start | bytes 65536 | tf_op jit(solution)/shard_map/all_to_all | solution.py:78
  50.1 7.3 %collective-permute-start.1 = (f32[327,1,128]{2,0,1:T(8,128)S(1)}, f32[327,1,128]{2,0,1:T(8,128)S(1)}, u32[]{:S(2)}, u32[]{:S(2)}) collective-permute-start(f32[327,1,128]{2,0,1:T(8,128)S(1)} %copy.90), channel_id=1, source_target_pairs={{1,0},{2,1},{3,2},{4,3},{5,4},{6,5},{7,6},{9,8},{10,9},{11,10},{12... | collective-permute-start | bytes 502280 | tf_op jit(solution)/shard_map/ppermute | solution.py:21
  51.4 7.4 %collective-permute-start = (f32[327,1,128]{2,0,1:T(8,128)S(1)}, f32[327,1,128]{2,0,1:T(8,128)S(1)}, u32[]{:S(2)}, u32[]{:S(2)}) collective-permute-start(f32[327,1,128]{2,0,1:T(8,128)S(1)} %copy.89), channel_id=1, source_target_pairs={{0,1},{1,2},{2,3},{3,4},{4,5},{5,6},{6,7},{8,9},{9,10},{10,11},{11... | collective-permute-start | bytes 502280 | tf_op jit(solution)/shard_map/ppermute | solution.py:20
  65.3 7.7 %collective-permute-start.3 = (f32[327,1,128]{2,0,1:T(8,128)S(1)}, f32[327,1,128]{2,0,1:T(8,128)S(1)}, u32[]{:S(2)}, u32[]{:S(2)}) collective-permute-start(f32[327,1,128]{2,0,1:T(8,128)S(1)} %copy.97), channel_id=1, source_target_pairs={{1,0},{2,1},{3,2},{4,3},{5,4},{6,5},{7,6},{9,8},{10,9},{11,10},{12... | collective-permute-start | bytes 502280 | tf_op jit(solution)/shard_map/ppermute | solution.py:21
  66.7 8.9 %collective-permute-start.2 = (f32[327,1,128]{2,0,1:T(8,128)S(1)}, f32[327,1,128]{2,0,1:T(8,128)S(1)}, u32[]{:S(2)}, u32[]{:S(2)}) collective-permute-start(f32[327,1,128]{2,0,1:T(8,128)S(1)} %copy.96), channel_id=1, source_target_pairs={{0,1},{1,2},{2,3},{3,4},{4,5},{5,6},{6,7},{8,9},{9,10},{10,11},{11... | collective-permute-start | bytes 502280 | tf_op jit(solution)/shard_map/ppermute | solution.py:20
  82.1 7.9 %collective-permute-start.5 = (f32[327,1,128]{2,0,1:T(8,128)S(1)}, f32[327,1,128]{2,0,1:T(8,128)S(1)}, u32[]{:S(2)}, u32[]{:S(2)}) collective-permute-start(f32[327,1,128]{2,0,1:T(8,128)S(1)} %copy.104), channel_id=1, source_target_pairs={{1,0},{2,1},{3,2},{4,3},{5,4},{6,5},{7,6},{9,8},{10,9},{11,10},{12... | collective-permute-start | bytes 502280 | tf_op jit(solution)/shard_map/ppermute | solution.py:21
  83.4 9.7 %collective-permute-start.4 = (f32[327,1,128]{2,0,1:T(8,128)S(1)}, f32[327,1,128]{2,0,1:T(8,128)S(1)}, u32[]{:S(2)}, u32[]{:S(2)}) collective-permute-start(f32[327,1,128]{2,0,1:T(8,128)S(1)} %copy.103), channel_id=1, source_target_pairs={{0,1},{1,2},{2,3},{3,4},{4,5},{5,6},{6,7},{8,9},{9,10},{10,11},{11... | collective-permute-start | bytes 502280 | tf_op jit(solution)/shard_map/ppermute | solution.py:20
  99.4 20.7 %copy-start.2 = (f32[1,1024]{0,1:T(8,128)S(1)}, f32[1,1024]{0,1:T(8,128)}, u32[]{:S(2)}) copy-start(f32[1,1024]{0,1:T(8,128)} %copy.116) | copy-start | bytes 12292
  99.7 21.3 %collective-permute-start.7 = (f32[327,1,128]{2,0,1:T(8,128)S(1)}, f32[327,1,128]{2,0,1:T(8,128)S(1)}, u32[]{:S(2)}, u32[]{:S(2)}) collective-permute-start(f32[327,1,128]{2,0,1:T(8,128)S(1)} %copy.111), channel_id=1, source_target_pairs={{1,0},{2,1},{3,2},{4,3},{5,4},{6,5},{7,6},{9,8},{10,9},{11,10},{12... | collective-permute-start | bytes 502280 | tf_op jit(solution)/shard_map/ppermute | solution.py:21
  101.0 20.2 %collective-permute-start.6 = (f32[327,1,128]{2,0,1:T(8,128)S(1)}, f32[327,1,128]{2,0,1:T(8,128)S(1)}, u32[]{:S(2)}, u32[]{:S(2)}) collective-permute-start(f32[327,1,128]{2,0,1:T(8,128)S(1)} %copy.110), channel_id=1, source_target_pairs={{0,1},{1,2},{2,3},{3,4},{4,5},{5,6},{6,7},{8,9},{9,10},{10,11},{11... | collective-permute-start | bytes 502280 | tf_op jit(solution)/shard_map/ppermute | solution.py:20
  127.3 1.1 copy-start.1
  143.7 11.5 %all-to-all-start.2 = ((f32[3,8,256]{2,0,1:T(4,128)}), f32[3,8,256]{2,0,1:T(4,128)S(1)}, u32[]{:S(2)}, u32[]{:S(2)}) async-start(f32[3,8,256]{2,0,1:T(4,128)} %copy.118), calls=%async_computation.2 | async-start | bytes 65536 | tf_op jit(solution)/shard_map/all_to_all | solution.py:100
where the time goes:
time: 172 us; the launch traced here: 171 us
  other arithmetic  56.1 us (33%)
  starting transfers between devices  40.6 us (24%)
  local copies, waits for them, and re-layouts  36.1 us (21%)
  waiting for transfers between devices  26 us (15%)
  blocking collectives  10.1 us (6%)
    ppermute x4, starting transfers between devices, with_halo(): before = lax.ppermute(last, axis, up)  20 us
    scatter-add x1, other arithmetic, local(): totals = jnp.zeros((3, ocean_cells), jnp.float32).at[:, flat_index].add(a...  14 us
    scatter-add x1, other arithmetic, local(): counts = jnp.zeros((ocean_cells,), jnp.float32).at[flat_index].add(weight)  13.9 us
    psum x1, blocking collectives, local(): partial_value = lax.psum(partial_value, 'sect')  10.1 us
    gather x2, local copies, waits for them, and re-layouts, local(): answer = jnp.where(is_valid[None], surface[:, slot_index], 0.0)  9.19 us
    add x4, other arithmetic, advance(): jnp.maximum(face_y, 0.0) * energy[:, :-1]  8.24 us
    all_to_all x1, starting transfers between devices, local(): lax.all_to_all(requests.reshape(tile_count, capacity), 'tile', split_axis...  7.28 us
    all_to_all x1, waiting for transfers between devices, local(): lax.all_to_all(packed.reshape(3, tile_count, capacity), 'tile', split_axi...  6.68 us
  transfers between devices with their start and end apart: 11, of which 8 were waited for; matrix products, arithmetic and copies ran while one was open for 12% of the time, Pallas kernels for 0%

commit v1 on v0

v1 whole, which is shorter than its diff:
```python
import functools
import math

import jax
import jax.numpy as jnp
import numpy as np
from jax import lax
from jax.experimental import pallas as pl
from jax.experimental.pallas import tpu as pltpu
from jax.sharding import PartitionSpec as P

NDIR = 36
NFREQ = 36
STEPS = 4
CHUNKS = 6
UNROLL = 3
MESH = pl.DeviceIdType.MESH
F32 = jnp.float32
BF16 = jnp.bfloat16


def split_bf16(x):
    high = x.astype(BF16)
    return high, (x - high.astype(F32)).astype(BF16)


def lanes_of(x):
    return jnp.concatenate([x[j : j + 1] for j in range(x.shape[0])], axis=1)


def kernel(
    tiles,
    sects,
    cos_ref,
    sin_ref,
    courant_ref,
    ratio_ref,
    current_ref,
    elevation_ref,
    mask_ref,
    owner_ref,
    slot_ref,
    spectrum_ref,
    out_ref,
    stress_ref,
    table,
    energy,
    halo,
    flow,
    scalars,
    parts,
    cells,
    local_sem,
    out_sem,
    halo_send,
    halo_recv,
    table_send,
    table_recv,
    part_send,
    part_recv,
    cell_send,
    cell_recv,
):
    tile = lax.axis_index("tile")
    sect = lax.axis_index("sect")
    bins = spectrum_ref.shape[0]
    rows, columns = mask_ref.shape
    half = rows // 2
    ocean_rows = elevation_ref.shape[0]
    ocean_cells = ocean_rows * columns
    per = bins // CHUNKS
    has_up = tile < tiles - 1
    has_down = tile > 0
    up = lax.rem(tile + 1, tiles)
    down = lax.rem(tile + tiles - 1, tiles)

    load = pltpu.make_async_copy(spectrum_ref, energy, local_sem)
    load.start()

    barrier = pltpu.get_barrier_semaphore()

    @pl.loop(1, tiles)
    def _(k):
        pl.semaphore_signal(
            barrier, inc=1, device_id=(sect, lax.rem(tile + k, tiles)), device_id_type=MESH
        )

    @pl.loop(1, sects)
    def _(k):
        pl.semaphore_signal(
            barrier, inc=1, device_id=(lax.rem(sect + k, sects), tile), device_id_type=MESH
        )

    for r in range(ocean_rows):
        at = pl.ds(r * columns, columns)
        table[tile, pl.ds(r, 1), :] = current_ref[pl.ds(0, 1), at]
        table[tile, pl.ds(ocean_rows + r, 1), :] = current_ref[pl.ds(1, 1), at]
    first = 3 * ocean_rows
    table[tile, pl.ds(2 * ocean_rows, ocean_rows), :] = elevation_ref[...]
    table[tile, pl.ds(first, rows), :] = (owner_ref[...] * ocean_cells + slot_ref[...]).astype(F32)
    table[tile, pl.ds(first + rows, rows), :] = mask_ref[...].astype(F32)

    pl.semaphore_wait(barrier, tiles + sects - 2)

    def table_copy(k, slot):
        return pltpu.make_async_remote_copy(
            src_ref=table.at[tile],
            dst_ref=table.at[slot],
            send_sem=table_send.at[k],
            recv_sem=table_recv.at[slot],
            device_id=(sect, lax.rem(tile + k, tiles)),
            device_id_type=MESH,
        )

    @pl.loop(1, tiles)
    def _(k):
        table_copy(k, tile).start()

    def halo_copy(side, c):
        at = (pl.ds(c * per, per), pl.ds(side * half, half))
        return pltpu.make_async_remote_copy(
            src_ref=spectrum_ref.at[at],
            dst_ref=halo.at[at],
            send_sem=halo_send.at[side, c],
            recv_sem=halo_recv.at[side, c],
            device_id=(sect, down if side == 0 else up),
            device_id_type=MESH,
        )

    for c in range(CHUNKS):

        @pl.when(has_down)
        def _():
            halo_copy(0, c).start()

        @pl.when(has_up)
        def _():
            halo_copy(1, c).start()

    @pl.loop(0, bins)
    def _(b):
        number = sect * bins + b
        d = number // NFREQ
        f = number % NFREQ
        c = cos_ref[d]
        s = sin_ref[d]
        g = courant_ref[f]
        n = ratio_ref[f]
        scale = 4.0 / (NDIR * NFREQ)
        scalars[0, b] = g * c
        scalars[1, b] = g * s
        scalars[2, b] = (n * (1.0 + c * c) - 0.5) * scale
        scalars[3, b] = (n * c * s) * scale
        scalars[4, b] = (n * (1.0 + s * s) - 0.5) * scale

    @pl.loop(1, tiles)
    def _(k):
        table_copy(k, lax.rem(tile + tiles - k, tiles)).wait_recv()

    sub = lax.broadcasted_iota(jnp.int32, (rows, columns), 0)
    upper = sub < half
    valid = (upper & has_up) | (jnp.logical_not(upper) & has_down)

    def ring(start):
        own = table[tile, pl.ds(start, rows), :]
        other = jnp.where(
            upper, table[up, pl.ds(start, rows), :], table[down, pl.ds(start, rows), :]
        )
        return own, other

    target_own, target_halo = ring(first)
    mask_own, mask_halo = ring(first + rows)
    mask_halo = jnp.where(valid, mask_halo, 0.0)
    target_own = target_own.astype(jnp.int32)
    target_halo = target_halo.astype(jnp.int32)

    table_rows = tiles * ocean_rows
    pieces = []
    for field in range(3):
        whole = table[:, pl.ds(field * ocean_rows, ocean_rows), :].reshape(table_rows, columns)
        high, low = split_bf16(whole.T)
        pieces.append(jnp.concatenate([high, low], axis=1))
    lookup = jnp.concatenate(pieces, axis=0)
    row_ids = lax.broadcasted_iota(jnp.int32, (table_rows, 2 * columns), 0)
    lane_ids = lax.broadcasted_iota(jnp.int32, (columns, 2 * columns), 0)
    for j in range(rows):
        index = jnp.concatenate([target_own[j : j + 1], target_halo[j : j + 1]], axis=1)
        hot = jnp.where(row_ids == index // columns, 1.0, 0.0).astype(BF16)
        found = jnp.dot(
            lookup, jnp.concatenate([hot, hot], axis=0), preferred_element_type=F32
        )
        chosen = lane_ids == index % columns
        for field in range(3):
            value = jnp.sum(
                jnp.where(chosen, found[field * columns : (field + 1) * columns], 0.0),
                axis=0,
                keepdims=True,
            )
            flow[field, pl.ds(j, 1), :] = value

    def north(own, other):
        a = pltpu.roll(own, rows - 1, 0)
        b = pltpu.roll(other, rows - 1, 0)
        edge = sub == rows - 1
        return jnp.where(edge, b, a), jnp.where(edge, a, b)

    def south(own, other):
        a = pltpu.roll(own, 1, 0)
        b = pltpu.roll(other, 1, 0)
        edge = sub == 0
        return jnp.where(edge, b, a), jnp.where(edge, a, b)

    def east(x):
        return pltpu.roll(x, columns - 1, 1)

    def west(x):
        return pltpu.roll(x, 1, 1)

    u_own = flow[0, :, pl.ds(0, columns)]
    u_halo = jnp.where(valid, flow[0, :, pl.ds(columns, columns)], 0.0)
    v_own = flow[1, :, pl.ds(0, columns)]
    v_halo = jnp.where(valid, flow[1, :, pl.ds(columns, columns)], 0.0)
    factor = (1.0 + flow[2, :, pl.ds(0, columns)]) * mask_own
    ux_own = 0.5 * (u_own + east(u_own))
    ux_halo = 0.5 * (u_halo + east(u_halo))
    vn_own, vn_halo = north(v_own, v_halo)
    vy_own = 0.5 * (v_own + vn_own)
    vy_halo = 0.5 * (v_halo + vn_halo)

    def one_bin(b):
        e_own = energy[b]
        e_halo = jnp.where(valid, halo[b], 0.0)
        sx = scalars[0, b]
        sy = scalars[1, b]
        ax_own, ax_halo = sx + ux_own, sx + ux_halo
        ay_own, ay_halo = sy + vy_own, sy + vy_halo
        xp_own, xm_own = jnp.maximum(ax_own, 0.0), jnp.minimum(ax_own, 0.0)
        xp_halo, xm_halo = jnp.maximum(ax_halo, 0.0), jnp.minimum(ax_halo, 0.0)
        yp_own, ym_own = jnp.maximum(ay_own, 0.0), jnp.minimum(ay_own, 0.0)
        yp_halo, ym_halo = jnp.maximum(ay_halo, 0.0), jnp.minimum(ay_halo, 0.0)
        for step in range(STEPS):
            n_own, n_halo = north(e_own, e_halo)
            fy_own = yp_own * e_own + ym_own * n_own
            fy_halo = yp_halo * e_halo + ym_halo * n_halo
            s_own, s_halo = south(fy_own, fy_halo)
            fx_own = xp_own * e_own + xm_own * east(e_own)
            if step < STEPS - 1:
                fx_halo = xp_halo * e_halo + xm_halo * east(e_halo)
                e_halo = mask_halo * (e_halo - (fx_halo - west(fx_halo)) - (fy_halo - s_halo))
            e_own = mask_own * (e_own - (fx_own - west(fx_own)) - (fy_own - s_own))
        energy[b] = e_own
        return e_own

    load.wait()
    sums = (jnp.zeros((rows, columns), F32),) * 3
    stores = []
    for c in range(CHUNKS):

        @pl.when(has_up)
        def _():
            halo_copy(0, c).wait_recv()

        @pl.when(has_down)
        def _():
            halo_copy(1, c).wait_recv()

        def body(i, carry):
            for k in range(UNROLL):
                b = c * per + i * UNROLL + k
                e = one_bin(b)
                carry = tuple(carry[q] + scalars[2 + q, b] * e for q in range(3))
            return carry

        sums = lax.fori_loop(0, per // UNROLL, body, sums)
        at = pl.ds(c * per, per)
        store = pltpu.make_async_copy(energy.at[at], out_ref.at[at], out_sem.at[c])
        store.start()
        stores.append(store)

    def part_copy(k, slot):
        return pltpu.make_async_remote_copy(
            src_ref=parts.at[sect],
            dst_ref=parts.at[slot],
            send_sem=part_send.at[k],
            recv_sem=part_recv.at[slot],
            device_id=(lax.rem(sect + k, sects), tile),
            device_id_type=MESH,
        )

    parts[sect] = jnp.concatenate(sums, axis=0)
    for k in range(1, sects):
        part_copy(k, sect).start()
    for k in range(1, sects):
        part_copy(k, lax.rem(sect + sects - k, sects)).wait_recv()
    total = parts[0]
    for k in range(1, sects):
        total = total + parts[k]
    cells[tile] = total * jnp.concatenate([factor] * 3, axis=0)

    def cell_copy(k, slot):
        return pltpu.make_async_remote_copy(
            src_ref=cells.at[tile],
            dst_ref=cells.at[slot],
            send_sem=cell_send.at[k],
            recv_sem=cell_recv.at[slot],
            device_id=(sect, lax.rem(tile + k, tiles)),
            device_id_type=MESH,
        )

    @pl.loop(1, tiles)
    def _(k):
        cell_copy(k, tile).start()

    cell_count = rows * columns
    ocean_ids = lax.broadcasted_iota(jnp.int32, (ocean_rows, cell_count), 0)
    column_ids = lax.broadcasted_iota(jnp.int32, (columns, cell_count), 0)

    def add_tile(source, acc):
        index = lanes_of(table[source, pl.ds(first, rows), :].astype(jnp.int32))
        stress = cells[source]
        row_hot = ocean_ids == index // columns - tile * ocean_rows
        lane_hot = jnp.where(column_ids == index % columns, 1.0, 0.0).astype(BF16)
        highs, lows = [], []
        for k in range(3):
            value = jnp.where(row_hot, lanes_of(stress[k * rows : (k + 1) * rows]), 0.0)
            high, low = split_bf16(value)
            highs.append(high)
            lows.append(low)
        ones = jnp.where(row_hot, 1.0, 0.0).astype(BF16)
        left = jnp.concatenate(highs + lows + [ones], axis=0)
        return acc + lax.dot_general(
            left, lane_hot, (((1,), (1,)), ((), ())), preferred_element_type=F32
        )

    acc = add_tile(tile, jnp.zeros((7 * ocean_rows, columns), F32))

    def add_other(k, acc):
        source = lax.rem(tile + tiles - k, tiles)
        cell_copy(k, source).wait_recv()
        return add_tile(source, acc)

    acc = lax.fori_loop(1, tiles, add_other, acc)
    counts = jnp.maximum(acc[6 * ocean_rows :], 1.0)
    for k in range(3):
        high = acc[k * ocean_rows : (k + 1) * ocean_rows]
        low = acc[(3 + k) * ocean_rows : (4 + k) * ocean_rows]
        mean = (high + low) / counts
        for r in range(ocean_rows):
            stress_ref[pl.ds(k, 1), pl.ds(r * columns, columns)] = mean[r : r + 1]

    for store in stores:
        store.wait()
    for c in range(CHUNKS):

        @pl.when(has_down)
        def _():
            halo_copy(0, c).wait_send()

        @pl.when(has_up)
        def _():
            halo_copy(1, c).wait_send()

    for k in range(1, sects):
        part_copy(k, sect).wait_send()

    @pl.loop(1, tiles)
    def _(k):
        table_copy(k, tile).wait_send()
        cell_copy(k, tile).wait_send()


def local(
    spectrum, courant, group_ratio, ocean_currents, elevation, sea_mask, owner_tile, ocean_slot
):
    bins, rows, columns = spectrum.shape
    tiles = lax.axis_size("tile")
    sects = lax.axis_size("sect")
    ocean_rows = elevation.shape[0] // columns
    angles = (np.arange(NDIR) + 0.5) * (2.0 * math.pi / NDIR)
    smem = pl.BlockSpec(memory_space=pltpu.SMEM)
    vmem = pl.BlockSpec(memory_space=pltpu.VMEM)
    anywhere = pl.BlockSpec(memory_space=pl.ANY)
    dma = pltpu.SemaphoreType.DMA
    return pl.pallas_call(
        functools.partial(kernel, tiles, sects),
        out_shape=(
            jax.ShapeDtypeStruct(spectrum.shape, F32),
            jax.ShapeDtypeStruct((3, elevation.shape[0]), F32),
        ),
        in_specs=[smem] * 4 + [vmem] * 5 + [anywhere],
        out_specs=(anywhere, vmem),
        scratch_shapes=[
            pltpu.VMEM((tiles, 3 * ocean_rows + 2 * rows, columns), F32),
            pltpu.VMEM(spectrum.shape, F32),
            pltpu.VMEM(spectrum.shape, F32),
            pltpu.VMEM((3, rows, 2 * columns), F32),
            pltpu.SMEM((5, bins), F32),
            pltpu.VMEM((sects, 3 * rows, columns), F32),
            pltpu.VMEM((tiles, 3 * rows, columns), F32),
            dma,
            dma((CHUNKS,)),
            dma((2, CHUNKS)),
            dma((2, CHUNKS)),
            dma((tiles,)),
            dma((tiles,)),
            dma((sects,)),
            dma((sects,)),
            dma((tiles,)),
            dma((tiles,)),
        ],
        compiler_params=pltpu.CompilerParams(
            collective_id=0, has_side_effects=True, vmem_limit_bytes=48 * 1024 * 1024
        ),
        cost_estimate=pl.CostEstimate(
            flops=bins * rows * columns * 200, bytes_accessed=8 * bins * rows * columns,
            transcendentals=0,
        ),
        name="coupling",
    )(
        jnp.asarray(np.cos(angles), F32),
        jnp.asarray(np.sin(angles), F32),
        courant,
        group_ratio,
        ocean_currents,
        elevation.reshape(ocean_rows, columns),
        sea_mask,
        owner_tile.reshape(rows, columns),
        ocean_slot.reshape(rows, columns),
        spectrum,
    )


def solution(mesh):
    in_specs = (
        P("sect", "tile", None),
        P(),
        P(),
        P(None, "tile"),
        P("tile"),
        P("tile", None),
        P("tile", None),
        P("tile"),
    )
    out_specs = (P("sect", "tile", None), P(None, "tile"))
    return jax.shard_map(local, mesh=mesh, in_specs=in_specs, out_specs=out_specs, check_vma=False)
```

time: 172 us -> 110 us (0.64)
  Pallas kernels: 0 us -> 100 us
  other arithmetic: 56.1 us -> 0 us
  starting transfers between devices: 40.6 us -> 0 us
  local copies, waits for them, and re-layouts: 36.1 us -> 9.08 us
  waiting for transfers between devices: 26 us -> 0 us
  blocking collectives: 10.1 us -> 0 us
    pallas_call x0 -> x1, Pallas kernels: none -> 100 us  [local(): pl.pallas_call(functools.partial(kernel, tiles, sects), out_shape=(jax.Sh...]
    scatter-add x2 -> x0, other arithmetic: 27.9 us -> none  [the longest x1 14 us: local(): totals = jnp.zeros((3, ocean_cells), jnp.float32).at[:, flat_index].add(a...]
    ppermute x8 -> x0, starting transfers between devices: 25.2 us -> none  [the longest x4 20 us: with_halo(): before = lax.ppermute(last, axis, up)]
    all_to_all x3 -> x0, waiting for transfers between devices: 17.3 us -> none  [the longest x1 6.68 us: local(): lax.all_to_all(packed.reshape(3, tile_count, capacity), 'tile', split_axi...]
    add x15 -> x0, other arithmetic: 15.6 us -> none  [the longest x4 8.24 us: advance(): jnp.maximum(face_y, 0.0) * energy[:, :-1]]
    all_to_all x3 -> x0, starting transfers between devices: 15.4 us -> none  [the longest x1 7.28 us: local(): lax.all_to_all(requests.reshape(tile_count, capacity), 'tile', split_axis...]
    gather x3 -> x0, local copies, waits for them, and re-layouts: 13.2 us -> none  [the longest x2 9.19 us: local(): answer = jnp.where(is_valid[None], surface[:, slot_index], 0.0)]
    psum x1 -> x0, blocking collectives: 10.1 us -> none  [local(): partial_value = lax.psum(partial_value, 'sect')]
  transfers between devices with their start and end apart: 11 -> 0, of which waited for: 8 -> 0; matrix products, arithmetic and copies ran while one was open for 12% -> 0% of each run, Pallas kernels for 0% -> 0%
where the time goes in v1:
time: 110 us
  Pallas kernels  100 us (91%)
  local copies, waits for them, and re-layouts  9.08 us (8%)
    pallas_call x1, Pallas kernels, local(): pl.pallas_call(functools.partial(kernel, tiles, sects), out_shape=(jax.Sh...  100 us
    unnamed x22, local copies, waits for them, and re-layouts  9.08 us

profile of v1, /device:TPU:0, one launch (start us, length us, event | category | flops | bytes accessed | tf_op | source)
XLA Modules:
  0.0 109.8 jit_solution(13657894820279540756)
XLA Ops:
  0.6 0.0 copy-start
  0.6 1.3 %copy-done = f32[324,8,128]{2,1,0:T(8,128)S(1)} copy-done((f32[324,8,128]{2,1,0:T(8,128)S(1)}, f32[324,8,128]{2,1,0:T(8,128)}, u32[]{:S(2)}) %copy-start) | copy-done | bytes 1327128
  2.0 0.0 copy-start.1
  2.0 0.7 copy-done.1
  2.7 0.0 copy-start.2
  2.7 0.7 copy-done.2
  3.4 0.0 copy-start.3
  3.4 0.7 copy-done.3
  4.1 0.0 copy-start.4
  4.1 0.7 copy-done.4
  4.7 0.0 copy-start.5
  4.7 0.7 copy-done.5
  5.4 0.0 copy-start.6
  5.4 0.7 copy-done.6
  6.1 0.0 copy-start.7
  6.1 0.7 copy-done.7
  6.7 0.0 copy-start.8
  6.7 0.7 copy-done.8
  7.4 0.0 copy-start.9
  7.4 0.7 copy-done.9
  8.1 100.1 %coupling.1 = (f32[324,8,128]{2,1,0:T(8,128)S(1)}, f32[3,2048]{1,0:T(4,128)S(1)}) custom-call(f32[36]{0:T(128)S(1)} %copy-done.9, f32[36]{0:T(128)S(1)} %copy-done.8, f32[36]{0:T(128)S(1)} %copy-done.6, f32[36]{0:T(128)S(1)} %copy-done.7, f32[2,2048]{1,0:T(2,128)S(1)} %copy-done.1, f32[16,128]{1,0:T(8,128)S(1)} %bitcast.3, s32[8,128]{1,0:T(8,128)S(1)} %copy-done.3, ...), custom_call_target="tpu_custom_call" | custom-call | flops 66355200 | bytes 2654208 | tf_op jit(solution)/shard_map/coupling/pallas_call | solution.py:384
  108.2 1.1 copy.14
  109.2 0.6 copy.15
Async XLA Ops:
  0.6 1.3 %copy-start = (f32[324,8,128]{2,1,0:T(8,128)S(1)}, f32[324,8,128]{2,1,0:T(8,128)}, u32[]{:S(2)}) copy-start(f32[324,8,128]{2,1,0:T(8,128)} %spectrum_ref.1) | copy-start | bytes 3981316
  2.0 0.7 copy-start.1
  2.7 0.7 copy-start.2
  3.4 0.7 copy-start.3
  4.1 0.7 copy-start.4
  4.7 0.7 copy-start.5
  5.4 0.7 copy-start.6
  6.1 0.7 copy-start.7
  6.7 0.7 copy-start.8
  7.4 0.7 copy-start.9

commit v2 on v1

--- a/solution.py
+++ b/solution.py
@@ -12,8 +12,8 @@
 NDIR = 36
 NFREQ = 36
 STEPS = 4
-CHUNKS = 6
-UNROLL = 3
+CHUNKS = 8
+GROUP = 8
 MESH = pl.DeviceIdType.MESH
 F32 = jnp.float32
 BF16 = jnp.bfloat16
@@ -28,29 +28,43 @@
     return jnp.concatenate([x[j : j + 1] for j in range(x.shape[0])], axis=1)
 
 
+def chunk_bounds(groups):
+    return [groups * c // CHUNKS for c in range(CHUNKS + 1)]
+
+
 def kernel(
     tiles,
     sects,
-    cos_ref,
-    sin_ref,
+    trig_hbm,
+    courant_hbm,
+    ratio_hbm,
+    current_hbm,
+    elevation_hbm,
+    mask_hbm,
+    owner_hbm,
+    slot_hbm,
+    spectrum_ref,
+    out_ref,
+    stress_ref,
+    trig_ref,
     courant_ref,
     ratio_ref,
     current_ref,
-    elevation_ref,
     mask_ref,
     owner_ref,
     slot_ref,
-    spectrum_ref,
-    out_ref,
-    stress_ref,
     table,
     energy,
+    result,
     halo,
     flow,
+    fields,
     scalars,
+    sums,
     parts,
     cells,
-    local_sem,
+    small_sem,
+    load_sem,
     out_sem,
     halo_send,
     halo_recv,
@@ -66,15 +80,31 @@
     bins = spectrum_ref.shape[0]
     rows, columns = mask_ref.shape
     half = rows // 2
-    ocean_rows = elevation_ref.shape[0]
+    ocean_rows = elevation_hbm.shape[0]
     ocean_cells = ocean_rows * columns
-    per = bins // CHUNKS
+    groups = halo.shape[0] // GROUP
+    bounds = chunk_bounds(groups)
+    first = 3 * ocean_rows
+    shift = columns.bit_length() - 1
     has_up = tile < tiles - 1
     has_down = tile > 0
     up = lax.rem(tile + 1, tiles)
     down = lax.rem(tile + tiles - 1, tiles)
 
-    load = pltpu.make_async_copy(spectrum_ref, energy, local_sem)
+    small = [
+        (trig_hbm, trig_ref),
+        (courant_hbm, courant_ref),
+        (ratio_hbm, ratio_ref),
+        (current_hbm, current_ref),
+        (elevation_hbm, table.at[tile, pl.ds(2 * ocean_rows, ocean_rows)]),
+        (mask_hbm, mask_ref),
+        (owner_hbm, owner_ref),
+        (slot_hbm, slot_ref),
+    ]
+    small = [pltpu.make_async_copy(a, b, small_sem.at[i]) for i, (a, b) in enumerate(small)]
+    for copy in small:
+        copy.start()
+    load = pltpu.make_async_copy(spectrum_ref, energy.at[pl.ds(0, bins)], load_sem)
     load.start()
 
     barrier = pltpu.get_barrier_semaphore()
@@ -91,12 +121,12 @@
             barrier, inc=1, device_id=(lax.rem(sect + k, sects), tile), device_id_type=MESH
         )
 
+    for copy in small:
+        copy.wait()
     for r in range(ocean_rows):
         at = pl.ds(r * columns, columns)
         table[tile, pl.ds(r, 1), :] = current_ref[pl.ds(0, 1), at]
         table[tile, pl.ds(ocean_rows + r, 1), :] = current_ref[pl.ds(1, 1), at]
-    first = 3 * ocean_rows
-    table[tile, pl.ds(2 * ocean_rows, ocean_rows), :] = elevation_ref[...]
     table[tile, pl.ds(first, rows), :] = (owner_ref[...] * ocean_cells + slot_ref[...]).astype(F32)
     table[tile, pl.ds(first + rows, rows), :] = mask_ref[...].astype(F32)
 
@@ -117,7 +147,8 @@
         table_copy(k, tile).start()
 
     def halo_copy(side, c):
-        at = (pl.ds(c * per, per), pl.ds(side * half, half))
+        begin, end = bounds[c] * GROUP, min(bounds[c + 1] * GROUP, bins)
+        at = (pl.ds(begin, end - begin), pl.ds(side * half, half))
         return pltpu.make_async_remote_copy(
             src_ref=spectrum_ref.at[at],
             dst_ref=halo.at[at],
@@ -137,21 +168,35 @@
         def _():
             halo_copy(1, c).start()
 
-    @pl.loop(0, bins)
-    def _(b):
-        number = sect * bins + b
-        d = number // NFREQ
-        f = number % NFREQ
-        c = cos_ref[d]
-        s = sin_ref[d]
+    def fill(b, place):
+        d, f = place
+        c = trig_ref[d]
+        s = trig_ref[NDIR + d]
         g = courant_ref[f]
         n = ratio_ref[f]
         scale = 4.0 / (NDIR * NFREQ)
-        scalars[0, b] = g * c
-        scalars[1, b] = g * s
-        scalars[2, b] = (n * (1.0 + c * c) - 0.5) * scale
-        scalars[3, b] = (n * c * s) * scale
-        scalars[4, b] = (n * (1.0 + s * s) - 0.5) * scale
+        values = (
+            g * c,
+            g * s,
+            (n * (1.0 + c * c) - 0.5) * scale,
+            (n * c * s) * scale,
+            (n * (1.0 + s * s) - 0.5) * scale,
+        )
+        for q in range(5):
+            scalars[q, pl.ds(b, 1), :] = jnp.full((1, columns), values[q], F32)
+        last = f == NFREQ - 1
+        return jnp.where(last, d + 1, d), jnp.where(last, 0, f + 1)
+
+    start = sect * bins
+    lax.fori_loop(0, bins, fill, (start // NFREQ, start % NFREQ))
+    spare = groups * GROUP - bins
+    if spare:
+        for q in range(5):
+            scalars[q, pl.ds(bins, spare), :] = jnp.zeros((spare, columns), F32)
+        for b in range(bins, bins + spare):
+            energy[b] = jnp.zeros((rows, columns), F32)
+            halo[b] = jnp.zeros((rows, columns), F32)
+    sums[...] = jnp.zeros_like(sums)
 
     @pl.loop(1, tiles)
     def _(k):
@@ -185,11 +230,11 @@
     lane_ids = lax.broadcasted_iota(jnp.int32, (columns, 2 * columns), 0)
     for j in range(rows):
         index = jnp.concatenate([target_own[j : j + 1], target_halo[j : j + 1]], axis=1)
-        hot = jnp.where(row_ids == index // columns, 1.0, 0.0).astype(BF16)
+        hot = jnp.where(row_ids == index >> shift, 1.0, 0.0).astype(BF16)
         found = jnp.dot(
             lookup, jnp.concatenate([hot, hot], axis=0), preferred_element_type=F32
         )
-        chosen = lane_ids == index % columns
+        chosen = lane_ids == (index & (columns - 1))
         for field in range(3):
             value = jnp.sum(
                 jnp.where(chosen, found[field * columns : (field + 1) * columns], 0.0),
@@ -198,18 +243,6 @@
             )
             flow[field, pl.ds(j, 1), :] = value
 
-    def north(own, other):
-        a = pltpu.roll(own, rows - 1, 0)
-        b = pltpu.roll(other, rows - 1, 0)
-        edge = sub == rows - 1
-        return jnp.where(edge, b, a), jnp.where(edge, a, b)
-
-    def south(own, other):
-        a = pltpu.roll(own, 1, 0)
-        b = pltpu.roll(other, 1, 0)
-        edge = sub == 0
-        return jnp.where(edge, b, a), jnp.where(edge, a, b)
-
     def east(x):
         return pltpu.roll(x, columns - 1, 1)
 
@@ -221,38 +254,69 @@
     v_own = flow[1, :, pl.ds(0, columns)]
     v_halo = jnp.where(valid, flow[1, :, pl.ds(columns, columns)], 0.0)
     factor = (1.0 + flow[2, :, pl.ds(0, columns)]) * mask_own
-    ux_own = 0.5 * (u_own + east(u_own))
-    ux_halo = 0.5 * (u_halo + east(u_halo))
-    vn_own, vn_halo = north(v_own, v_halo)
-    vy_own = 0.5 * (v_own + vn_own)
-    vy_halo = 0.5 * (v_halo + vn_halo)
-
-    def one_bin(b):
-        e_own = energy[b]
-        e_halo = jnp.where(valid, halo[b], 0.0)
-        sx = scalars[0, b]
-        sy = scalars[1, b]
-        ax_own, ax_halo = sx + ux_own, sx + ux_halo
-        ay_own, ay_halo = sy + vy_own, sy + vy_halo
-        xp_own, xm_own = jnp.maximum(ax_own, 0.0), jnp.minimum(ax_own, 0.0)
-        xp_halo, xm_halo = jnp.maximum(ax_halo, 0.0), jnp.minimum(ax_halo, 0.0)
-        yp_own, ym_own = jnp.maximum(ay_own, 0.0), jnp.minimum(ay_own, 0.0)
-        yp_halo, ym_halo = jnp.maximum(ay_halo, 0.0), jnp.minimum(ay_halo, 0.0)
-        for step in range(STEPS):
-            n_own, n_halo = north(e_own, e_halo)
-            fy_own = yp_own * e_own + ym_own * n_own
-            fy_halo = yp_halo * e_halo + ym_halo * n_halo
-            s_own, s_halo = south(fy_own, fy_halo)
-            fx_own = xp_own * e_own + xm_own * east(e_own)
-            if step < STEPS - 1:
-                fx_halo = xp_halo * e_halo + xm_halo * east(e_halo)
-                e_halo = mask_halo * (e_halo - (fx_halo - west(fx_halo)) - (fy_halo - s_halo))
-            e_own = mask_own * (e_own - (fx_own - west(fx_own)) - (fy_own - s_own))
-        energy[b] = e_own
-        return e_own
+    extent = rows + 2 * half
+
+    def in_order(own, other):
+        return jnp.concatenate([other[half:], own, other[:half]], axis=0)
+
+    u_all = in_order(u_own, u_halo)
+    v_all = in_order(v_own, v_halo)
+    m_all = in_order(mask_own, mask_halo)
+    ux_all = 0.5 * (u_all + east(u_all))
+    uw_all = west(ux_all)
+    vy_all = 0.5 * (v_all[:-1] + v_all[1:])
+    for j in range(extent):
+        fields[0, j] = jnp.broadcast_to(ux_all[j : j + 1], (GROUP, columns))
+        fields[1, j] = jnp.broadcast_to(uw_all[j : j + 1], (GROUP, columns))
+        fields[2, j] = jnp.broadcast_to(m_all[j : j + 1], (GROUP, columns))
+        if j < extent - 1:
+            fields[3, j] = jnp.broadcast_to(vy_all[j : j + 1], (GROUP, columns))
+
+    lines = bins + spare
+    energy_rows = energy.reshape(lines * rows, columns)
+    halo_rows = halo.reshape(lines * rows, columns)
+    result_rows = result.reshape(lines * rows, columns)
+
+    def one_group(g, _):
+        begin = g * GROUP
+        base = begin * rows
+        e = {}
+        for j in range(rows):
+            place = base + j
+            e[half + j] = energy_rows[pl.ds(place, GROUP, stride=rows), :]
+            outside = halo_rows[pl.ds(place, GROUP, stride=rows), :]
+            if j < half:
+                e[half + rows + j] = jnp.where(has_up, outside, 0.0)
+            else:
+                e[j - half] = jnp.where(has_down, outside, 0.0)
+        sx = scalars[0, pl.ds(begin, GROUP), :]
+        sy = scalars[1, pl.ds(begin, GROUP), :]
+        yp, ym, xm, xpw, c0 = {}, {}, {}, {}, {}
+        for j in range(extent - 1):
+            ay = sy + fields[3, j]
+            yp[j], ym[j] = jnp.maximum(ay, 0.0), jnp.minimum(ay, 0.0)
+        for j in range(1, extent - 1):
+            ax = sx + fields[0, j]
+            aw = sx + fields[1, j]
+            xm[j] = jnp.minimum(ax, 0.0)
+            xpw[j] = jnp.maximum(aw, 0.0)
+            c0[j] = (1.0 - jnp.maximum(ax, 0.0) + jnp.minimum(aw, 0.0)) - (yp[j] - ym[j - 1])
+        for step in range(1, STEPS + 1):
+            new = {}
+            for j in range(step, extent - step):
+                value = c0[j] * e[j] - xm[j] * east(e[j]) + xpw[j] * west(e[j])
+                value = value - ym[j] * e[j + 1] + yp[j - 1] * e[j - 1]
+                new[j] = fields[2, j] * value
+            e = new
+        weights = [scalars[2 + k, pl.ds(begin, GROUP), :] for k in range(3)]
+        for j in range(rows):
+            final = e[half + j]
+            result_rows[pl.ds(base + j, GROUP, stride=rows), :] = final
+            for k in range(3):
+                sums[k, j] += weights[k] * final
+        return 0
 
     load.wait()
-    sums = (jnp.zeros((rows, columns), F32),) * 3
     stores = []
     for c in range(CHUNKS):
 
@@ -264,16 +328,10 @@
         def _():
             halo_copy(1, c).wait_recv()
 
-        def body(i, carry):
-            for k in range(UNROLL):
-                b = c * per + i * UNROLL + k
-                e = one_bin(b)
-                carry = tuple(carry[q] + scalars[2 + q, b] * e for q in range(3))
-            return carry
-
-        sums = lax.fori_loop(0, per // UNROLL, body, sums)
-        at = pl.ds(c * per, per)
-        store = pltpu.make_async_copy(energy.at[at], out_ref.at[at], out_sem.at[c])
+        lax.fori_loop(bounds[c], bounds[c + 1], one_group, 0)
+        begin, end = bounds[c] * GROUP, min(bounds[c + 1] * GROUP, bins)
+        at = pl.ds(begin, end - begin)
+        store = pltpu.make_async_copy(result.at[at], out_ref.at[at], out_sem.at[c])
         store.start()
         stores.append(store)
 
@@ -287,7 +345,9 @@
             device_id_type=MESH,
         )
 
-    parts[sect] = jnp.concatenate(sums, axis=0)
+    for k in range(3):
+        for j in range(rows):
+            parts[sect, pl.ds(k * rows + j, 1), :] = jnp.sum(sums[k, j], axis=0, keepdims=True)
     for k in range(1, sects):
         part_copy(k, sect).start()
     for k in range(1, sects):
@@ -318,8 +378,8 @@
     def add_tile(source, acc):
         index = lanes_of(table[source, pl.ds(first, rows), :].astype(jnp.int32))
         stress = cells[source]
-        row_hot = ocean_ids == index // columns - tile * ocean_rows
-        lane_hot = jnp.where(column_ids == index % columns, 1.0, 0.0).astype(BF16)
+        row_hot = ocean_ids == (index >> shift) - tile * ocean_rows
+        lane_hot = jnp.where(column_ids == (index & (columns - 1)), 1.0, 0.0).astype(BF16)
         highs, lows = [], []
         for k in range(3):
             value = jnp.where(row_hot, lanes_of(stress[k * rows : (k + 1) * rows]), 0.0)
@@ -377,9 +437,10 @@
     sects = lax.axis_size("sect")
     ocean_rows = elevation.shape[0] // columns
     angles = (np.arange(NDIR) + 0.5) * (2.0 * math.pi / NDIR)
-    smem = pl.BlockSpec(memory_space=pltpu.SMEM)
+    lines = -(-bins // GROUP) * GROUP
+    extent = 2 * rows
     vmem = pl.BlockSpec(memory_space=pltpu.VMEM)
-    anywhere = pl.BlockSpec(memory_space=pl.ANY)
+    hbm = pl.BlockSpec(memory_space=pltpu.HBM)
     dma = pltpu.SemaphoreType.DMA
     return pl.pallas_call(
         functools.partial(kernel, tiles, sects),
@@ -387,16 +448,27 @@
             jax.ShapeDtypeStruct(spectrum.shape, F32),
             jax.ShapeDtypeStruct((3, elevation.shape[0]), F32),
         ),
-        in_specs=[smem] * 4 + [vmem] * 5 + [anywhere],
-        out_specs=(anywhere, vmem),
+        in_specs=[hbm] * 9,
+        out_specs=(hbm, vmem),
         scratch_shapes=[
+            pltpu.SMEM((2 * NDIR,), F32),
+            pltpu.SMEM((NFREQ,), F32),
+            pltpu.SMEM((NFREQ,), F32),
+            pltpu.VMEM(ocean_currents.shape, F32),
+            pltpu.VMEM((rows, columns), jnp.int32),
+            pltpu.VMEM((rows, columns), jnp.int32),
+            pltpu.VMEM((rows, columns), jnp.int32),
             pltpu.VMEM((tiles, 3 * ocean_rows + 2 * rows, columns), F32),
-            pltpu.VMEM(spectrum.shape, F32),
-            pltpu.VMEM(spectrum.shape, F32),
+            pltpu.VMEM((lines, rows, columns), F32),
+            pltpu.VMEM((lines, rows, columns), F32),
+            pltpu.VMEM((lines, rows, columns), F32),
             pltpu.VMEM((3, rows, 2 * columns), F32),
-            pltpu.SMEM((5, bins), F32),
+            pltpu.VMEM((4, extent, GROUP, columns), F32),
+            pltpu.VMEM((5, lines, columns), F32),
+            pltpu.VMEM((3, rows, GROUP, columns), F32),
             pltpu.VMEM((sects, 3 * rows, columns), F32),
             pltpu.VMEM((tiles, 3 * rows, columns), F32),
+            dma((8,)),
             dma,
             dma((CHUNKS,)),
             dma((2, CHUNKS)),
@@ -409,7 +481,7 @@
             dma((tiles,)),
         ],
         compiler_params=pltpu.CompilerParams(
-            collective_id=0, has_side_effects=True, vmem_limit_bytes=48 * 1024 * 1024
+            collective_id=0, has_side_effects=True, vmem_limit_bytes=60 * 1024 * 1024
         ),
         cost_estimate=pl.CostEstimate(
             flops=bins * rows * columns * 200, bytes_accessed=8 * bins * rows * columns,
@@ -417,8 +489,7 @@
         ),
         name="coupling",
     )(
-        jnp.asarray(np.cos(angles), F32),
-        jnp.asarray(np.sin(angles), F32),
+        jnp.asarray(np.concatenate([np.cos(angles), np.sin(angles)]), F32),
         courant,
         group_ratio,
         ocean_currents,

time: 110 us -> 54.5 us (0.50)
  Pallas kernels: 100 us -> 50.6 us
  local copies, waits for them, and re-layouts: 9.08 us -> 3.09 us
    pallas_call x1, Pallas kernels: 100 us -> 50.6 us  [local(): pl.pallas_call(functools.partial(kernel, tiles, sects), out_shape=(jax.Sh...]
    unnamed x22 -> x4, local copies, waits for them, and re-layouts: 9.08 us -> 3.09 us
where the time goes in v2:
time: 54.5 us; the launch traced here: 54.4 us
  Pallas kernels  50.6 us (93%)
  local copies, waits for them, and re-layouts  3.09 us (6%)
  between operations  0.65 us (1%)
    pallas_call x1, Pallas kernels, local(): pl.pallas_call(functools.partial(kernel, tiles, sects), out_shape=(jax.Sh...  50.6 us
    unnamed x4, local copies, waits for them, and re-layouts  3.09 us

profile of v2, /device:TPU:0, one launch (start us, length us, event | category | flops | bytes accessed | tf_op | source)
XLA Modules:
  0.0 54.4 jit_solution(6520709157354218672)
XLA Ops:
  0.6 50.6 %coupling.1 = (f32[324,8,128]{2,1,0:T(8,128)}, f32[3,2048]{1,0:T(4,128)}) custom-call(f32[72]{0:T(128)} %constant.2.clone.trig_hbm, f32[36]{0:T(128)} %courant_hbm.1, f32[36]{0:T(128)} %ratio_hbm.1, f32[2,2048]{1,0:T(2,128)} %current_hbm.1, f32[16,128]{1,0:T(8,128)} %bitcast.3, s32[8,128]{1,0:T(8,128)} %mask_hbm.1, s32[8,128]{1,0:T(8,128)} %bitcast.4, ...), custom_call_target="tpu_custom_call" | custom-call | flops 66355200 | bytes 2654208 | tf_op jit(solution)/shard_map/coupling/pallas_call | solution.py:445
  51.3 0.0 copy-start
  51.3 2.5 %copy.13 = f32[324,8,128]{2,1,0:T(8,128)} copy(f32[324,8,128]{2,1,0:T(8,128)} %get-tuple-element.4) | data formatting | bytes 2654208
  53.7 0.0 copy-done
  53.7 0.6 %copy.14 = f32[3,2048]{1,0:T(4,128)} copy(f32[3,2048]{1,0:T(4,128)S(1)} %copy-done) | data formatting | bytes 49152
Async XLA Ops:
  51.3 2.5 %copy-start = (f32[3,2048]{1,0:T(4,128)S(1)}, f32[3,2048]{1,0:T(4,128)}, u32[]{:S(2)}) copy-start(f32[3,2048]{1,0:T(4,128)} %get-tuple-element.5) | copy-start | bytes 73732

commit v3 on v2

--- a/solution.py
+++ b/solution.py
@@ -13,6 +13,7 @@
 NFREQ = 36
 STEPS = 4
 CHUNKS = 8
+SHARES = (0, 6, 12, 18, 24, 30, 35, 39, 41)
 GROUP = 8
 MESH = pl.DeviceIdType.MESH
 F32 = jnp.float32
@@ -29,7 +30,7 @@
 
 
 def chunk_bounds(groups):
-    return [groups * c // CHUNKS for c in range(CHUNKS + 1)]
+    return [groups * share // SHARES[-1] for share in SHARES]
 
 
 def kernel(
@@ -60,6 +61,8 @@
     flow,
     fields,
     scalars,
+    by_freq,
+    hots,
     sums,
     parts,
     cells,
@@ -168,27 +171,30 @@
         def _():
             halo_copy(1, c).start()
 
-    def fill(b, place):
-        d, f = place
-        c = trig_ref[d]
-        s = trig_ref[NDIR + d]
-        g = courant_ref[f]
-        n = ratio_ref[f]
-        scale = 4.0 / (NDIR * NFREQ)
+    start = sect * bins
+    first_dir, first_freq = start // NFREQ, start % NFREQ
+    for i in range(NFREQ):
+        f = first_freq + i
+        f = jnp.where(f >= NFREQ, f - NFREQ, f)
+        by_freq[0, pl.ds(i, 1), :] = jnp.full((1, columns), courant_ref[f], F32)
+        by_freq[1, pl.ds(i, 1), :] = jnp.full((1, columns), ratio_ref[f], F32)
+    speed, ratio = by_freq[0], by_freq[1]
+    wrapped = lax.broadcasted_iota(jnp.int32, (NFREQ, columns), 0) + first_freq >= NFREQ
+    scale = 4.0 / (NDIR * NFREQ)
+    for begin in range(0, bins, NFREQ):
+        count = min(NFREQ, bins - begin)
+        d = first_dir + begin // NFREQ
+        c = jnp.where(wrapped, trig_ref[d + 1], trig_ref[d])
+        s = jnp.where(wrapped, trig_ref[NDIR + d + 1], trig_ref[NDIR + d])
         values = (
-            g * c,
-            g * s,
-            (n * (1.0 + c * c) - 0.5) * scale,
-            (n * c * s) * scale,
-            (n * (1.0 + s * s) - 0.5) * scale,
+            speed * c,
+            speed * s,
+            (ratio * (1.0 + c * c) - 0.5) * scale,
+            (ratio * c * s) * scale,
+            (ratio * (1.0 + s * s) - 0.5) * scale,
         )
         for q in range(5):
-            scalars[q, pl.ds(b, 1), :] = jnp.full((1, columns), values[q], F32)
-        last = f == NFREQ - 1
-        return jnp.where(last, d + 1, d), jnp.where(last, 0, f + 1)
-
-    start = sect * bins
-    lax.fori_loop(0, bins, fill, (start // NFREQ, start % NFREQ))
+            scalars[q, pl.ds(begin, count), :] = values[q][:count]
     spare = groups * GROUP - bins
     if spare:
         for q in range(5):
@@ -292,22 +298,30 @@
         sx = scalars[0, pl.ds(begin, GROUP), :]
         sy = scalars[1, pl.ds(begin, GROUP), :]
         yp, ym, xm, xpw, c0 = {}, {}, {}, {}, {}
-        for j in range(extent - 1):
+
+        def coefficients(j):
             ay = sy + fields[3, j]
             yp[j], ym[j] = jnp.maximum(ay, 0.0), jnp.minimum(ay, 0.0)
-        for j in range(1, extent - 1):
-            ax = sx + fields[0, j]
-            aw = sx + fields[1, j]
-            xm[j] = jnp.minimum(ax, 0.0)
-            xpw[j] = jnp.maximum(aw, 0.0)
-            c0[j] = (1.0 - jnp.maximum(ax, 0.0) + jnp.minimum(aw, 0.0)) - (yp[j] - ym[j - 1])
-        for step in range(1, STEPS + 1):
-            new = {}
-            for j in range(step, extent - step):
-                value = c0[j] * e[j] - xm[j] * east(e[j]) + xpw[j] * west(e[j])
-                value = value - ym[j] * e[j + 1] + yp[j - 1] * e[j - 1]
-                new[j] = fields[2, j] * value
-            e = new
+            if j:
+                ax = sx + fields[0, j]
+                aw = sx + fields[1, j]
+                xm[j] = jnp.minimum(ax, 0.0)
+                xpw[j] = jnp.maximum(aw, 0.0)
+                c0[j] = (1.0 - jnp.maximum(ax, 0.0) + jnp.minimum(aw, 0.0)) - (yp[j] - ym[j - 1])
+
+        levels = [e] + [{} for _ in range(STEPS)]
+        coefficients(0)
+        for wave in range(1, extent + 2 * STEPS):
+            if wave < extent - 1:
+                coefficients(wave)
+            for step in range(STEPS, 0, -1):
+                j = wave - 2 * (step - 1)
+                if step <= j < extent - step:
+                    old = levels[step - 1]
+                    value = c0[j] * old[j] - xm[j] * east(old[j]) + xpw[j] * west(old[j])
+                    value = value - ym[j] * old[j + 1] + yp[j - 1] * old[j - 1]
+                    levels[step][j] = fields[2, j] * value
+        e = levels[STEPS]
         weights = [scalars[2 + k, pl.ds(begin, GROUP), :] for k in range(3)]
         for j in range(rows):
             final = e[half + j]
@@ -350,6 +364,22 @@
             parts[sect, pl.ds(k * rows + j, 1), :] = jnp.sum(sums[k, j], axis=0, keepdims=True)
     for k in range(1, sects):
         part_copy(k, sect).start()
+
+    cell_count = rows * columns
+    ocean_ids = lax.broadcasted_iota(jnp.int32, (ocean_rows, cell_count), 0) + tile * ocean_rows
+
+    def index_of(source):
+        return lanes_of(table[source, pl.ds(first, rows), :].astype(jnp.int32))
+
+    def row_hot_of(source):
+        return ocean_ids == index_of(source) >> shift
+
+    @pl.loop(0, tiles)
+    def _(source):
+        lane = index_of(source) & (columns - 1)
+        ids = lax.broadcasted_iota(jnp.int32, (columns, cell_count), 0)
+        hots[source] = jnp.where(ids == lane, 1.0, 0.0).astype(BF16)
+
     for k in range(1, sects):
         part_copy(k, lax.rem(sect + sects - k, sects)).wait_recv()
     total = parts[0]
@@ -371,28 +401,28 @@
     def _(k):
         cell_copy(k, tile).start()
 
-    cell_count = rows * columns
-    ocean_ids = lax.broadcasted_iota(jnp.int32, (ocean_rows, cell_count), 0)
-    column_ids = lax.broadcasted_iota(jnp.int32, (columns, cell_count), 0)
+    def product(left, source):
+        return lax.dot_general(
+            left, hots[source], (((1,), (1,)), ((), ())), preferred_element_type=F32
+        )
+
+    def count_tile(source, counts):
+        return counts + product(jnp.where(row_hot_of(source), 1.0, 0.0).astype(BF16), source)
+
+    counts = lax.fori_loop(0, tiles, count_tile, jnp.zeros((ocean_rows, columns), F32))
 
     def add_tile(source, acc):
-        index = lanes_of(table[source, pl.ds(first, rows), :].astype(jnp.int32))
         stress = cells[source]
-        row_hot = ocean_ids == (index >> shift) - tile * ocean_rows
-        lane_hot = jnp.where(column_ids == (index & (columns - 1)), 1.0, 0.0).astype(BF16)
+        row_hot = row_hot_of(source)
         highs, lows = [], []
         for k in range(3):
-            value = jnp.where(row_hot, lanes_of(stress[k * rows : (k + 1) * rows]), 0.0)
-            high, low = split_bf16(value)
-            highs.append(high)
-            lows.append(low)
-        ones = jnp.where(row_hot, 1.0, 0.0).astype(BF16)
-        left = jnp.concatenate(highs + lows + [ones], axis=0)
-        return acc + lax.dot_general(
-            left, lane_hot, (((1,), (1,)), ((), ())), preferred_element_type=F32
-        )
-
-    acc = add_tile(tile, jnp.zeros((7 * ocean_rows, columns), F32))
+            high, low = split_bf16(stress[k * rows : (k + 1) * rows])
+            for value, into in ((high, highs), (low, lows)):
+                value = lanes_of(value.astype(F32))
+                into.append(jnp.where(row_hot, value, 0.0).astype(BF16))
+        return acc + product(jnp.concatenate(highs + lows, axis=0), source)
+
+    acc = add_tile(tile, jnp.zeros((6 * ocean_rows, columns), F32))
 
     def add_other(k, acc):
         source = lax.rem(tile + tiles - k, tiles)
@@ -400,7 +430,7 @@
         return add_tile(source, acc)
 
     acc = lax.fori_loop(1, tiles, add_other, acc)
-    counts = jnp.maximum(acc[6 * ocean_rows :], 1.0)
+    counts = jnp.maximum(counts, 1.0)
     for k in range(3):
         high = acc[k * ocean_rows : (k + 1) * ocean_rows]
         low = acc[(3 + k) * ocean_rows : (4 + k) * ocean_rows]
@@ -451,7 +481,7 @@
         in_specs=[hbm] * 9,
         out_specs=(hbm, vmem),
         scratch_shapes=[
-            pltpu.SMEM((2 * NDIR,), F32),
+            pltpu.SMEM((2 * NDIR + 8,), F32),
             pltpu.SMEM((NFREQ,), F32),
             pltpu.SMEM((NFREQ,), F32),
             pltpu.VMEM(ocean_currents.shape, F32),
@@ -465,6 +495,8 @@
             pltpu.VMEM((3, rows, 2 * columns), F32),
             pltpu.VMEM((4, extent, GROUP, columns), F32),
             pltpu.VMEM((5, lines, columns), F32),
+            pltpu.VMEM((2, NFREQ, columns), F32),
+            pltpu.VMEM((tiles, columns, rows * columns), BF16),
             pltpu.VMEM((3, rows, GROUP, columns), F32),
             pltpu.VMEM((sects, 3 * rows, columns), F32),
             pltpu.VMEM((tiles, 3 * rows, columns), F32),
@@ -489,7 +521,7 @@
         ),
         name="coupling",
     )(
-        jnp.asarray(np.concatenate([np.cos(angles), np.sin(angles)]), F32),
+        jnp.asarray(np.concatenate([np.cos(angles), np.sin(angles), np.zeros(8)]), F32),
         courant,
         group_ratio,
         ocean_currents,

time: 54.5 us -> 54.8 us (level)
  no operation moved by 1% of the time
where the time goes in v3:
time: 54.8 us; the launch traced here: 54.6 us
  Pallas kernels  50.9 us (93%)
  local copies, waits for them, and re-layouts  3.09 us (6%)
  between operations  0.65 us (1%)
    pallas_call x1, Pallas kernels, local(): pl.pallas_call(functools.partial(kernel, tiles, sects), out_shape=(jax.Sh...  50.9 us
    unnamed x4, local copies, waits for them, and re-layouts  3.09 us

profile of v3, /device:TPU:0, one launch (start us, length us, event | category | flops | bytes accessed | tf_op | source)
XLA Modules:
  0.0 54.6 jit_solution(8746787369119218909)
XLA Ops:
  0.6 50.9 %coupling.1 = (f32[324,8,128]{2,1,0:T(8,128)}, f32[3,2048]{1,0:T(4,128)}) custom-call(f32[80]{0:T(128)} %constant.2.clone.trig_hbm, f32[36]{0:T(128)} %courant_hbm.1, f32[36]{0:T(128)} %ratio_hbm.1, f32[2,2048]{1,0:T(2,128)} %current_hbm.1, f32[16,128]{1,0:T(8,128)} %bitcast.3, s32[8,128]{1,0:T(8,128)} %mask_hbm.1, s32[8,128]{1,0:T(8,128)} %bitcast.4, ...), custom_call_target="tpu_custom_call" | custom-call | flops 66355200 | bytes 2654208 | tf_op jit(solution)/shard_map/coupling/pallas_call | solution.py:475
  51.5 0.0 copy-start
  51.5 2.5 %copy.13 = f32[324,8,128]{2,1,0:T(8,128)} copy(f32[324,8,128]{2,1,0:T(8,128)} %get-tuple-element.4) | data formatting | bytes 2654208
  54.0 0.0 copy-done
  54.0 0.6 %copy.14 = f32[3,2048]{1,0:T(4,128)} copy(f32[3,2048]{1,0:T(4,128)S(1)} %copy-done) | data formatting | bytes 49152
Async XLA Ops:
  51.5 2.5 %copy-start = (f32[3,2048]{1,0:T(4,128)S(1)}, f32[3,2048]{1,0:T(4,128)}, u32[]{:S(2)}) copy-start(f32[3,2048]{1,0:T(4,128)} %get-tuple-element.5) | copy-start | bytes 73732

commit v4 on v3

--- a/solution.py
+++ b/solution.py
@@ -54,8 +54,10 @@
     mask_ref,
     owner_ref,
     slot_ref,
+    bundle,
     table,
     energy,
+    packed,
     result,
     halo,
     flow,
@@ -73,6 +75,8 @@
     halo_recv,
     table_send,
     table_recv,
+    forward_send,
+    forward_recv,
     part_send,
     part_recv,
     cell_send,
@@ -85,7 +89,7 @@
     half = rows // 2
     ocean_rows = elevation_hbm.shape[0]
     ocean_cells = ocean_rows * columns
-    groups = halo.shape[0] // GROUP
+    groups = halo.shape[1] // GROUP
     bounds = chunk_bounds(groups)
     first = 3 * ocean_rows
     shift = columns.bit_length() - 1
@@ -94,12 +98,15 @@
     up = lax.rem(tile + 1, tiles)
     down = lax.rem(tile + tiles - 1, tiles)
 
+    load = pltpu.make_async_copy(spectrum_ref, energy.at[pl.ds(0, bins)], load_sem)
+    load.start()
+
     small = [
         (trig_hbm, trig_ref),
         (courant_hbm, courant_ref),
         (ratio_hbm, ratio_ref),
         (current_hbm, current_ref),
-        (elevation_hbm, table.at[tile, pl.ds(2 * ocean_rows, ocean_rows)]),
+        (elevation_hbm, bundle.at[pl.ds(2 * ocean_rows, ocean_rows)]),
         (mask_hbm, mask_ref),
         (owner_hbm, owner_ref),
         (slot_hbm, slot_ref),
@@ -107,9 +114,6 @@
     small = [pltpu.make_async_copy(a, b, small_sem.at[i]) for i, (a, b) in enumerate(small)]
     for copy in small:
         copy.start()
-    load = pltpu.make_async_copy(spectrum_ref, energy.at[pl.ds(0, bins)], load_sem)
-    load.start()
-
     barrier = pltpu.get_barrier_semaphore()
 
     @pl.loop(1, tiles)
@@ -124,36 +128,25 @@
             barrier, inc=1, device_id=(lax.rem(sect + k, sects), tile), device_id_type=MESH
         )
 
-    for copy in small:
-        copy.wait()
-    for r in range(ocean_rows):
-        at = pl.ds(r * columns, columns)
-        table[tile, pl.ds(r, 1), :] = current_ref[pl.ds(0, 1), at]
-        table[tile, pl.ds(ocean_rows + r, 1), :] = current_ref[pl.ds(1, 1), at]
-    table[tile, pl.ds(first, rows), :] = (owner_ref[...] * ocean_cells + slot_ref[...]).astype(F32)
-    table[tile, pl.ds(first + rows, rows), :] = mask_ref[...].astype(F32)
-
-    pl.semaphore_wait(barrier, tiles + sects - 2)
-
-    def table_copy(k, slot):
+    lines = groups * GROUP
+    spare = lines - bins
+    energy_rows = energy.reshape(lines * rows, columns)
+    result_rows = result.reshape(lines * rows, columns)
+    for b in range(bins, lines):
+        energy[b] = jnp.zeros((rows, columns), F32)
+
+    def pack(g, _):
+        for r in range(rows):
+            packed[r, pl.ds(g * GROUP, GROUP), :] = energy_rows[
+                pl.ds(g * GROUP * rows + r, GROUP, stride=rows), :
+            ]
+        return 0
+
+    def halo_copy(side, c):
+        begin, end = bounds[c] * GROUP, bounds[c + 1] * GROUP
+        at = (pl.ds(side * half, half), pl.ds(begin, end - begin))
         return pltpu.make_async_remote_copy(
-            src_ref=table.at[tile],
-            dst_ref=table.at[slot],
-            send_sem=table_send.at[k],
-            recv_sem=table_recv.at[slot],
-            device_id=(sect, lax.rem(tile + k, tiles)),
-            device_id_type=MESH,
-        )
-
-    @pl.loop(1, tiles)
-    def _(k):
-        table_copy(k, tile).start()
-
-    def halo_copy(side, c):
-        begin, end = bounds[c] * GROUP, min(bounds[c + 1] * GROUP, bins)
-        at = (pl.ds(begin, end - begin), pl.ds(side * half, half))
-        return pltpu.make_async_remote_copy(
-            src_ref=spectrum_ref.at[at],
+            src_ref=packed.at[at],
             dst_ref=halo.at[at],
             send_sem=halo_send.at[side, c],
             recv_sem=halo_recv.at[side, c],
@@ -161,8 +154,7 @@
             device_id_type=MESH,
         )
 
-    for c in range(CHUNKS):
-
+    def send_chunk(c):
         @pl.when(has_down)
         def _():
             halo_copy(0, c).start()
@@ -170,6 +162,52 @@
         @pl.when(has_up)
         def _():
             halo_copy(1, c).start()
+
+    load.wait()
+    lax.fori_loop(bounds[0], bounds[1], pack, 0)
+    pl.semaphore_wait(barrier, tiles + sects - 2)
+    send_chunk(0)
+
+    for copy in small:
+        copy.wait()
+    for r in range(ocean_rows):
+        at = pl.ds(r * columns, columns)
+        bundle[pl.ds(r, 1), :] = current_ref[pl.ds(0, 1), at]
+        bundle[pl.ds(ocean_rows + r, 1), :] = current_ref[pl.ds(1, 1), at]
+    bundle[pl.ds(first, rows), :] = (owner_ref[...] * ocean_cells + slot_ref[...]).astype(F32)
+    bundle[pl.ds(first + rows, rows), :] = mask_ref[...].astype(F32)
+    share = bundle.shape[0] // sects
+    piece = pl.ds(pl.multiple_of(sect * share, 8), share)
+    table[tile, piece, :] = bundle[piece, :]
+
+    def table_copy(k, slot):
+        return pltpu.make_async_remote_copy(
+            src_ref=bundle.at[piece],
+            dst_ref=table.at[slot, piece],
+            send_sem=table_send.at[k],
+            recv_sem=table_recv.at[slot],
+            device_id=(sect, lax.rem(tile + k, tiles)),
+            device_id_type=MESH,
+        )
+
+    def forward_copy(k, source):
+        at = pl.ds(pl.multiple_of(source * share, 8), share)
+        return pltpu.make_async_remote_copy(
+            src_ref=table.at[:, at],
+            dst_ref=table.at[:, at],
+            send_sem=forward_send.at[k],
+            recv_sem=forward_recv.at[source],
+            device_id=(lax.rem(sect + k, sects), tile),
+            device_id_type=MESH,
+        )
+
+    @pl.loop(1, tiles)
+    def _(k):
+        table_copy(k, tile).start()
+
+    for c in range(1, CHUNKS):
+        lax.fori_loop(bounds[c], bounds[c + 1], pack, 0)
+        send_chunk(c)
 
     start = sect * bins
     first_dir, first_freq = start // NFREQ, start % NFREQ
@@ -195,18 +233,19 @@
         )
         for q in range(5):
             scalars[q, pl.ds(begin, count), :] = values[q][:count]
-    spare = groups * GROUP - bins
     if spare:
         for q in range(5):
             scalars[q, pl.ds(bins, spare), :] = jnp.zeros((spare, columns), F32)
-        for b in range(bins, bins + spare):
-            energy[b] = jnp.zeros((rows, columns), F32)
-            halo[b] = jnp.zeros((rows, columns), F32)
     sums[...] = jnp.zeros_like(sums)
 
     @pl.loop(1, tiles)
     def _(k):
         table_copy(k, lax.rem(tile + tiles - k, tiles)).wait_recv()
+
+    for k in range(1, sects):
+        forward_copy(k, sect).start()
+    for k in range(1, sects):
+        forward_copy(k, lax.rem(sect + sects - k, sects)).wait_recv()
 
     sub = lax.broadcasted_iota(jnp.int32, (rows, columns), 0)
     upper = sub < half
@@ -278,19 +317,13 @@
         if j < extent - 1:
             fields[3, j] = jnp.broadcast_to(vy_all[j : j + 1], (GROUP, columns))
 
-    lines = bins + spare
-    energy_rows = energy.reshape(lines * rows, columns)
-    halo_rows = halo.reshape(lines * rows, columns)
-    result_rows = result.reshape(lines * rows, columns)
-
     def one_group(g, _):
         begin = g * GROUP
         base = begin * rows
         e = {}
         for j in range(rows):
-            place = base + j
-            e[half + j] = energy_rows[pl.ds(place, GROUP, stride=rows), :]
-            outside = halo_rows[pl.ds(place, GROUP, stride=rows), :]
+            e[half + j] = packed[j, pl.ds(begin, GROUP), :]
+            outside = halo[j, pl.ds(begin, GROUP), :]
             if j < half:
                 e[half + rows + j] = jnp.where(has_up, outside, 0.0)
             else:
@@ -330,7 +363,6 @@
                 sums[k, j] += weights[k] * final
         return 0
 
-    load.wait()
     stores = []
     for c in range(CHUNKS):
 
@@ -452,6 +484,9 @@
 
     for k in range(1, sects):
         part_copy(k, sect).wait_send()
+
+    for k in range(1, sects):
+        forward_copy(k, sect).wait_send()
 
     @pl.loop(1, tiles)
     def _(k):
@@ -488,10 +523,12 @@
             pltpu.VMEM((rows, columns), jnp.int32),
             pltpu.VMEM((rows, columns), jnp.int32),
             pltpu.VMEM((rows, columns), jnp.int32),
+            pltpu.VMEM((3 * ocean_rows + 2 * rows, columns), F32),
             pltpu.VMEM((tiles, 3 * ocean_rows + 2 * rows, columns), F32),
             pltpu.VMEM((lines, rows, columns), F32),
+            pltpu.VMEM((rows, lines, columns), F32),
             pltpu.VMEM((lines, rows, columns), F32),
-            pltpu.VMEM((lines, rows, columns), F32),
+            pltpu.VMEM((rows, lines, columns), F32),
             pltpu.VMEM((3, rows, 2 * columns), F32),
             pltpu.VMEM((4, extent, GROUP, columns), F32),
             pltpu.VMEM((5, lines, columns), F32),
@@ -507,6 +544,8 @@
             dma((2, CHUNKS)),
             dma((tiles,)),
             dma((tiles,)),
+            dma((sects,)),
+            dma((sects,)),
             dma((sects,)),
             dma((sects,)),
             dma((tiles,)),

time: 54.8 us -> 56.8 us (1.036)
  Pallas kernels: 50.9 us -> 52.9 us
    pallas_call x1, Pallas kernels: 50.9 us -> 52.9 us  [local(): pl.pallas_call(functools.partial(kernel, tiles, sects), out_shape=(jax.Sh...]
where the time goes in v4:
time: 56.8 us; the launch traced here: 56.7 us
  Pallas kernels  52.9 us (93%)
  local copies, waits for them, and re-layouts  3.09 us (5%)
  between operations  0.65 us (1%)
    pallas_call x1, Pallas kernels, local(): pl.pallas_call(functools.partial(kernel, tiles, sects), out_shape=(jax.Sh...  52.9 us
    unnamed x4, local copies, waits for them, and re-layouts  3.09 us

profile of v4, /device:TPU:0, one launch (start us, length us, event | category | flops | bytes accessed | tf_op | source)
XLA Modules:
  0.0 56.7 jit_solution(14588372687186153408)
XLA Ops:
  0.6 52.9 %coupling.1 = (f32[324,8,128]{2,1,0:T(8,128)}, f32[3,2048]{1,0:T(4,128)}) custom-call(f32[80]{0:T(128)} %constant.2.clone.trig_hbm, f32[36]{0:T(128)} %courant_hbm.1, f32[36]{0:T(128)} %ratio_hbm.1, f32[2,2048]{1,0:T(2,128)} %current_hbm.1, f32[16,128]{1,0:T(8,128)} %bitcast.3, s32[8,128]{1,0:T(8,128)} %mask_hbm.1, s32[8,128]{1,0:T(8,128)} %bitcast.4, ...), custom_call_target="tpu_custom_call" | custom-call | flops 66355200 | bytes 2654208 | tf_op jit(solution)/shard_map/coupling/pallas_call | solution.py:510
  53.6 0.0 copy-start
  53.6 2.5 %copy.13 = f32[324,8,128]{2,1,0:T(8,128)} copy(f32[324,8,128]{2,1,0:T(8,128)} %get-tuple-element.4) | data formatting | bytes 2654208
  56.0 0.0 copy-done
  56.0 0.6 %copy.14 = f32[3,2048]{1,0:T(4,128)} copy(f32[3,2048]{1,0:T(4,128)S(1)} %copy-done) | data formatting | bytes 49152
Async XLA Ops:
  53.6 2.5 %copy-start = (f32[3,2048]{1,0:T(4,128)S(1)}, f32[3,2048]{1,0:T(4,128)}, u32[]{:S(2)}) copy-start(f32[3,2048]{1,0:T(4,128)} %get-tuple-element.5) | copy-start | bytes 73732

commit v5 on v3

--- a/solution.py
+++ b/solution.py
@@ -12,8 +12,8 @@
 NDIR = 36
 NFREQ = 36
 STEPS = 4
-CHUNKS = 8
-SHARES = (0, 6, 12, 18, 24, 30, 35, 39, 41)
+CHUNKS = 7
+ABREAST = 3
 GROUP = 8
 MESH = pl.DeviceIdType.MESH
 F32 = jnp.float32
@@ -27,10 +27,6 @@
 
 def lanes_of(x):
     return jnp.concatenate([x[j : j + 1] for j in range(x.shape[0])], axis=1)
-
-
-def chunk_bounds(groups):
-    return [groups * share // SHARES[-1] for share in SHARES]
 
 
 def kernel(
@@ -54,8 +50,10 @@
     mask_ref,
     owner_ref,
     slot_ref,
+    bundle,
     table,
     energy,
+    packed,
     result,
     halo,
     flow,
@@ -85,8 +83,8 @@
     half = rows // 2
     ocean_rows = elevation_hbm.shape[0]
     ocean_cells = ocean_rows * columns
-    groups = halo.shape[0] // GROUP
-    bounds = chunk_bounds(groups)
+    lines = halo.shape[1]
+    per = lines // CHUNKS
     first = 3 * ocean_rows
     shift = columns.bit_length() - 1
     has_up = tile < tiles - 1
@@ -94,12 +92,15 @@
     up = lax.rem(tile + 1, tiles)
     down = lax.rem(tile + tiles - 1, tiles)
 
+    load = pltpu.make_async_copy(spectrum_ref, energy.at[pl.ds(0, bins)], load_sem)
+    load.start()
+
     small = [
         (trig_hbm, trig_ref),
         (courant_hbm, courant_ref),
         (ratio_hbm, ratio_ref),
         (current_hbm, current_ref),
-        (elevation_hbm, table.at[tile, pl.ds(2 * ocean_rows, ocean_rows)]),
+        (elevation_hbm, bundle.at[pl.ds(2 * ocean_rows, ocean_rows)]),
         (mask_hbm, mask_ref),
         (owner_hbm, owner_ref),
         (slot_hbm, slot_ref),
@@ -107,9 +108,6 @@
     small = [pltpu.make_async_copy(a, b, small_sem.at[i]) for i, (a, b) in enumerate(small)]
     for copy in small:
         copy.start()
-    load = pltpu.make_async_copy(spectrum_ref, energy.at[pl.ds(0, bins)], load_sem)
-    load.start()
-
     barrier = pltpu.get_barrier_semaphore()
 
     @pl.loop(1, tiles)
@@ -124,20 +122,43 @@
             barrier, inc=1, device_id=(lax.rem(sect + k, sects), tile), device_id_type=MESH
         )
 
+    spare = lines - bins
+    energy_rows = energy.reshape(lines * rows, columns)
+    result_rows = result.reshape(lines * rows, columns)
+    for b in range(bins, lines):
+        energy[b] = jnp.zeros((rows, columns), F32)
+
+    def pack(g):
+        for r in range(rows):
+            packed[r, pl.ds(pl.multiple_of(g * GROUP, GROUP), GROUP), :] = energy_rows[
+                pl.ds(g * GROUP * rows + r, GROUP, stride=rows), :
+            ]
+
+    def halo_copy(side, c):
+        at = (pl.ds(side * half, half), pl.ds(pl.multiple_of(c * per, GROUP), per))
+        return pltpu.make_async_remote_copy(
+            src_ref=packed.at[at],
+            dst_ref=halo.at[at],
+            send_sem=halo_send.at[side, c],
+            recv_sem=halo_recv.at[side, c],
+            device_id=(sect, down if side == 0 else up),
+            device_id_type=MESH,
+        )
+
     for copy in small:
         copy.wait()
     for r in range(ocean_rows):
         at = pl.ds(r * columns, columns)
-        table[tile, pl.ds(r, 1), :] = current_ref[pl.ds(0, 1), at]
-        table[tile, pl.ds(ocean_rows + r, 1), :] = current_ref[pl.ds(1, 1), at]
-    table[tile, pl.ds(first, rows), :] = (owner_ref[...] * ocean_cells + slot_ref[...]).astype(F32)
-    table[tile, pl.ds(first + rows, rows), :] = mask_ref[...].astype(F32)
-
+        bundle[pl.ds(r, 1), :] = current_ref[pl.ds(0, 1), at]
+        bundle[pl.ds(ocean_rows + r, 1), :] = current_ref[pl.ds(1, 1), at]
+    bundle[pl.ds(first, rows), :] = (owner_ref[...] * ocean_cells + slot_ref[...]).astype(F32)
+    bundle[pl.ds(first + rows, rows), :] = mask_ref[...].astype(F32)
+    table[tile] = bundle[...]
     pl.semaphore_wait(barrier, tiles + sects - 2)
 
     def table_copy(k, slot):
         return pltpu.make_async_remote_copy(
-            src_ref=table.at[tile],
+            src_ref=bundle,
             dst_ref=table.at[slot],
             send_sem=table_send.at[k],
             recv_sem=table_recv.at[slot],
@@ -149,19 +170,12 @@
     def _(k):
         table_copy(k, tile).start()
 
-    def halo_copy(side, c):
-        begin, end = bounds[c] * GROUP, min(bounds[c + 1] * GROUP, bins)
-        at = (pl.ds(begin, end - begin), pl.ds(side * half, half))
-        return pltpu.make_async_remote_copy(
-            src_ref=spectrum_ref.at[at],
-            dst_ref=halo.at[at],
-            send_sem=halo_send.at[side, c],
-            recv_sem=halo_recv.at[side, c],
-            device_id=(sect, down if side == 0 else up),
-            device_id_type=MESH,
-        )
-
-    for c in range(CHUNKS):
+    load.wait()
+
+    @pl.loop(0, CHUNKS)
+    def _(c):
+        for g in range(per // GROUP):
+            pack(c * (per // GROUP) + g)
 
         @pl.when(has_down)
         def _():
@@ -170,6 +184,14 @@
         @pl.when(has_up)
         def _():
             halo_copy(1, c).start()
+
+    @pl.when(jnp.logical_not(has_up))
+    def _():
+        halo[pl.ds(0, half)] = jnp.zeros((half, lines, columns), F32)
+
+    @pl.when(jnp.logical_not(has_down))
+    def _():
+        halo[pl.ds(half, half)] = jnp.zeros((half, lines, columns), F32)
 
     start = sect * bins
     first_dir, first_freq = start // NFREQ, start % NFREQ
@@ -195,13 +217,9 @@
         )
         for q in range(5):
             scalars[q, pl.ds(begin, count), :] = values[q][:count]
-    spare = groups * GROUP - bins
     if spare:
         for q in range(5):
             scalars[q, pl.ds(bins, spare), :] = jnp.zeros((spare, columns), F32)
-        for b in range(bins, bins + spare):
-            energy[b] = jnp.zeros((rows, columns), F32)
-            halo[b] = jnp.zeros((rows, columns), F32)
     sums[...] = jnp.zeros_like(sums)
 
     @pl.loop(1, tiles)
@@ -278,62 +296,64 @@
         if j < extent - 1:
             fields[3, j] = jnp.broadcast_to(vy_all[j : j + 1], (GROUP, columns))
 
-    lines = bins + spare
-    energy_rows = energy.reshape(lines * rows, columns)
-    halo_rows = halo.reshape(lines * rows, columns)
-    result_rows = result.reshape(lines * rows, columns)
-
-    def one_group(g, _):
-        begin = g * GROUP
-        base = begin * rows
-        e = {}
-        for j in range(rows):
-            place = base + j
-            e[half + j] = energy_rows[pl.ds(place, GROUP, stride=rows), :]
-            outside = halo_rows[pl.ds(place, GROUP, stride=rows), :]
-            if j < half:
-                e[half + rows + j] = jnp.where(has_up, outside, 0.0)
-            else:
-                e[j - half] = jnp.where(has_down, outside, 0.0)
-        sx = scalars[0, pl.ds(begin, GROUP), :]
-        sy = scalars[1, pl.ds(begin, GROUP), :]
-        yp, ym, xm, xpw, c0 = {}, {}, {}, {}, {}
-
-        def coefficients(j):
-            ay = sy + fields[3, j]
-            yp[j], ym[j] = jnp.maximum(ay, 0.0), jnp.minimum(ay, 0.0)
+    class Group:
+        def __init__(self, begin):
+            begin = pl.multiple_of(begin, GROUP)
+            self.begin = begin
+            self.yp, self.ym, self.xm, self.xpw, self.c0 = {}, {}, {}, {}, {}
+            self.sx = scalars[0, pl.ds(begin, GROUP), :]
+            self.sy = scalars[1, pl.ds(begin, GROUP), :]
+            e = {}
+            for j in range(rows):
+                e[half + j] = packed[j, pl.ds(begin, GROUP), :]
+                e[half + rows + j if j < half else j - half] = halo[j, pl.ds(begin, GROUP), :]
+            self.levels = [e] + [{} for _ in range(STEPS)]
+
+        def coefficients(self, j):
+            ay = self.sy + fields[3, j]
+            self.yp[j], self.ym[j] = jnp.maximum(ay, 0.0), jnp.minimum(ay, 0.0)
             if j:
-                ax = sx + fields[0, j]
-                aw = sx + fields[1, j]
-                xm[j] = jnp.minimum(ax, 0.0)
-                xpw[j] = jnp.maximum(aw, 0.0)
-                c0[j] = (1.0 - jnp.maximum(ax, 0.0) + jnp.minimum(aw, 0.0)) - (yp[j] - ym[j - 1])
-
-        levels = [e] + [{} for _ in range(STEPS)]
-        coefficients(0)
+                ax = self.sx + fields[0, j]
+                aw = self.sx + fields[1, j]
+                self.xm[j] = jnp.minimum(ax, 0.0)
+                self.xpw[j] = jnp.maximum(aw, 0.0)
+                out_x = jnp.maximum(ax, 0.0) - jnp.minimum(aw, 0.0)
+                self.c0[j] = (1.0 - out_x) - (self.yp[j] - self.ym[j - 1])
+
+        def advance(self, step, j):
+            old = self.levels[step - 1]
+            value = self.c0[j] * old[j] - self.xm[j] * east(old[j]) + self.xpw[j] * west(old[j])
+            value = value - self.ym[j] * old[j + 1] + self.yp[j - 1] * old[j - 1]
+            self.levels[step][j] = fields[2, j] * value
+
+    def abreast(begin):
+        members = [Group(begin + i * GROUP) for i in range(ABREAST)]
+        for member in members:
+            member.coefficients(0)
         for wave in range(1, extent + 2 * STEPS):
-            if wave < extent - 1:
-                coefficients(wave)
+            for member in members:
+                if wave < extent - 1:
+                    member.coefficients(wave)
             for step in range(STEPS, 0, -1):
                 j = wave - 2 * (step - 1)
                 if step <= j < extent - step:
-                    old = levels[step - 1]
-                    value = c0[j] * old[j] - xm[j] * east(old[j]) + xpw[j] * west(old[j])
-                    value = value - ym[j] * old[j + 1] + yp[j - 1] * old[j - 1]
-                    levels[step][j] = fields[2, j] * value
-        e = levels[STEPS]
-        weights = [scalars[2 + k, pl.ds(begin, GROUP), :] for k in range(3)]
-        for j in range(rows):
-            final = e[half + j]
-            result_rows[pl.ds(base + j, GROUP, stride=rows), :] = final
-            for k in range(3):
-                sums[k, j] += weights[k] * final
-        return 0
-
-    load.wait()
-    stores = []
-    for c in range(CHUNKS):
-
+                    for member in members:
+                        member.advance(step, j)
+        for member in members:
+            for j in range(rows):
+                result_rows[pl.ds(member.begin * rows + j, GROUP, stride=rows), :] = (
+                    member.levels[STEPS][half + j]
+                )
+        for k in range(3):
+            weights = [scalars[2 + k, pl.ds(member.begin, GROUP), :] for member in members]
+            for j in range(rows):
+                added = sums[k, j]
+                for member, weight in zip(members, weights):
+                    added = added + weight * member.levels[STEPS][half + j]
+                sums[k, j] = added
+
+    @pl.loop(0, CHUNKS)
+    def _(c):
         @pl.when(has_up)
         def _():
             halo_copy(0, c).wait_recv()
@@ -342,12 +362,12 @@
         def _():
             halo_copy(1, c).wait_recv()
 
-        lax.fori_loop(bounds[c], bounds[c + 1], one_group, 0)
-        begin, end = bounds[c] * GROUP, min(bounds[c + 1] * GROUP, bins)
-        at = pl.ds(begin, end - begin)
-        store = pltpu.make_async_copy(result.at[at], out_ref.at[at], out_sem.at[c])
-        store.start()
-        stores.append(store)
+        @pl.loop(0, per // (GROUP * ABREAST))
+        def _(i):
+            abreast(c * per + i * (GROUP * ABREAST))
+
+    store = pltpu.make_async_copy(result.at[pl.ds(0, bins)], out_ref, out_sem)
+    store.start()
 
     def part_copy(k, slot):
         return pltpu.make_async_remote_copy(
@@ -438,8 +458,7 @@
         for r in range(ocean_rows):
             stress_ref[pl.ds(k, 1), pl.ds(r * columns, columns)] = mean[r : r + 1]
 
-    for store in stores:
-        store.wait()
+    store.wait()
     for c in range(CHUNKS):
 
         @pl.when(has_down)
@@ -467,7 +486,8 @@
     sects = lax.axis_size("sect")
     ocean_rows = elevation.shape[0] // columns
     angles = (np.arange(NDIR) + 0.5) * (2.0 * math.pi / NDIR)
-    lines = -(-bins // GROUP) * GROUP
+    unit = CHUNKS * ABREAST * GROUP
+    lines = -(-bins // unit) * unit
     extent = 2 * rows
     vmem = pl.BlockSpec(memory_space=pltpu.VMEM)
     hbm = pl.BlockSpec(memory_space=pltpu.HBM)
@@ -488,10 +508,12 @@
             pltpu.VMEM((rows, columns), jnp.int32),
             pltpu.VMEM((rows, columns), jnp.int32),
             pltpu.VMEM((rows, columns), jnp.int32),
+            pltpu.VMEM((3 * ocean_rows + 2 * rows, columns), F32),
             pltpu.VMEM((tiles, 3 * ocean_rows + 2 * rows, columns), F32),
             pltpu.VMEM((lines, rows, columns), F32),
+            pltpu.VMEM((rows, lines, columns), F32),
             pltpu.VMEM((lines, rows, columns), F32),
-            pltpu.VMEM((lines, rows, columns), F32),
+            pltpu.VMEM((rows, lines, columns), F32),
             pltpu.VMEM((3, rows, 2 * columns), F32),
             pltpu.VMEM((4, extent, GROUP, columns), F32),
             pltpu.VMEM((5, lines, columns), F32),
@@ -502,7 +524,7 @@
             pltpu.VMEM((tiles, 3 * rows, columns), F32),
             dma((8,)),
             dma,
-            dma((CHUNKS,)),
+            dma,
             dma((2, CHUNKS)),
             dma((2, CHUNKS)),
             dma((tiles,)),

time: 54.8 us -> 53.6 us (0.978)
  Pallas kernels: 50.9 us -> 49.7 us
    pallas_call x1, Pallas kernels: 50.9 us -> 49.7 us  [local(): pl.pallas_call(functools.partial(kernel, tiles, sects), out_shape=(jax.Sh...]
where the time goes in v5:
time: 53.6 us; the launch traced here: 53.4 us
  Pallas kernels  49.7 us (93%)
  local copies, waits for them, and re-layouts  3.09 us (6%)
  between operations  0.65 us (1%)
    pallas_call x1, Pallas kernels, local(): pl.pallas_call(functools.partial(kernel, tiles, sects), out_shape=(jax.Sh...  49.7 us
    unnamed x4, local copies, waits for them, and re-layouts  3.09 us

profile of v5, /device:TPU:0, one launch (start us, length us, event | category | flops | bytes accessed | tf_op | source)
XLA Modules:
  0.0 53.4 jit_solution(11505753440164154234)
XLA Ops:
  0.6 49.7 %coupling.1 = (f32[324,8,128]{2,1,0:T(8,128)}, f32[3,2048]{1,0:T(4,128)}) custom-call(f32[80]{0:T(128)} %constant.2.clone.trig_hbm, f32[36]{0:T(128)} %courant_hbm.1, f32[36]{0:T(128)} %ratio_hbm.1, f32[2,2048]{1,0:T(2,128)} %current_hbm.1, f32[16,128]{1,0:T(8,128)} %bitcast.3, s32[8,128]{1,0:T(8,128)} %mask_hbm.1, s32[8,128]{1,0:T(8,128)} %bitcast.4, ...), custom_call_target="tpu_custom_call" | custom-call | flops 66355200 | bytes 2654208 | tf_op jit(solution)/shard_map/coupling/pallas_call | solution.py:495
  50.3 0.0 copy-start
  50.3 2.5 %copy.13 = f32[324,8,128]{2,1,0:T(8,128)} copy(f32[324,8,128]{2,1,0:T(8,128)} %get-tuple-element.4) | data formatting | bytes 2654208
  52.8 0.0 copy-done
  52.8 0.6 %copy.14 = f32[3,2048]{1,0:T(4,128)} copy(f32[3,2048]{1,0:T(4,128)S(1)} %copy-done) | data formatting | bytes 49152
Async XLA Ops:
  50.3 2.5 %copy-start = (f32[3,2048]{1,0:T(4,128)S(1)}, f32[3,2048]{1,0:T(4,128)}, u32[]{:S(2)}) copy-start(f32[3,2048]{1,0:T(4,128)} %get-tuple-element.5) | copy-start | bytes 73732

commit v6 on v5

--- a/solution.py
+++ b/solution.py
@@ -15,6 +15,7 @@
 CHUNKS = 7
 ABREAST = 3
 GROUP = 8
+COPIES = 6
 MESH = pl.DeviceIdType.MESH
 F32 = jnp.float32
 BF16 = jnp.bfloat16
@@ -352,6 +353,32 @@
                     added = added + weight * member.levels[STEPS][half + j]
                 sums[k, j] = added
 
+    cell_count = rows * columns
+    ocean_ids = lax.broadcasted_iota(jnp.int32, (ocean_rows, cell_count), 0) + tile * ocean_rows
+
+    def index_of(source):
+        return lanes_of(table[source, pl.ds(first, rows), :].astype(jnp.int32))
+
+    def row_hot_of(source):
+        return ocean_ids == index_of(source) >> shift
+
+    @pl.loop(0, tiles)
+    def _(source):
+        lane = index_of(source) & (columns - 1)
+        ids = lax.broadcasted_iota(jnp.int32, (columns, cell_count), 0)
+        hots[source] = jnp.where(ids == lane, 1.0, 0.0).astype(BF16)
+
+    def product(left, source):
+        return lax.dot_general(
+            left, hots[source], (((1,), (1,)), ((), ())), preferred_element_type=F32
+        )
+
+    def count_tile(source, counts):
+        return counts + product(jnp.where(row_hot_of(source), 1.0, 0.0).astype(BF16), source)
+
+    counts = lax.fori_loop(0, tiles, count_tile, jnp.zeros((ocean_rows, columns), F32))
+    counts = jnp.maximum(counts, 1.0)
+
     @pl.loop(0, CHUNKS)
     def _(c):
         @pl.when(has_up)
@@ -385,21 +412,6 @@
     for k in range(1, sects):
         part_copy(k, sect).start()
 
-    cell_count = rows * columns
-    ocean_ids = lax.broadcasted_iota(jnp.int32, (ocean_rows, cell_count), 0) + tile * ocean_rows
-
-    def index_of(source):
-        return lanes_of(table[source, pl.ds(first, rows), :].astype(jnp.int32))
-
-    def row_hot_of(source):
-        return ocean_ids == index_of(source) >> shift
-
-    @pl.loop(0, tiles)
-    def _(source):
-        lane = index_of(source) & (columns - 1)
-        ids = lax.broadcasted_iota(jnp.int32, (columns, cell_count), 0)
-        hots[source] = jnp.where(ids == lane, 1.0, 0.0).astype(BF16)
-
     for k in range(1, sects):
         part_copy(k, lax.rem(sect + sects - k, sects)).wait_recv()
     total = parts[0]
@@ -420,16 +432,6 @@
     @pl.loop(1, tiles)
     def _(k):
         cell_copy(k, tile).start()
-
-    def product(left, source):
-        return lax.dot_general(
-            left, hots[source], (((1,), (1,)), ((), ())), preferred_element_type=F32
-        )
-
-    def count_tile(source, counts):
-        return counts + product(jnp.where(row_hot_of(source), 1.0, 0.0).astype(BF16), source)
-
-    counts = lax.fori_loop(0, tiles, count_tile, jnp.zeros((ocean_rows, columns), F32))
 
     def add_tile(source, acc):
         stress = cells[source]
@@ -450,7 +452,6 @@
         return add_tile(source, acc)
 
     acc = lax.fori_loop(1, tiles, add_other, acc)
-    counts = jnp.maximum(counts, 1.0)
     for k in range(3):
         high = acc[k * ocean_rows : (k + 1) * ocean_rows]
         low = acc[(3 + k) * ocean_rows : (4 + k) * ocean_rows]
@@ -476,6 +477,20 @@
     def _(k):
         table_copy(k, tile).wait_send()
         cell_copy(k, tile).wait_send()
+
+
+def hand_on(spectrum_ref, stress_ref, spectrum_out, stress_out, sems):
+    bins = spectrum_ref.shape[0]
+    copies = [pltpu.make_async_copy(stress_ref, stress_out, sems.at[COPIES])]
+    for i in range(COPIES):
+        at = pl.ds(bins * i // COPIES, bins * (i + 1) // COPIES - bins * i // COPIES)
+        copies.append(
+            pltpu.make_async_copy(spectrum_ref.at[at], spectrum_out.at[at], sems.at[i])
+        )
+    for copy in copies:
+        copy.start()
+    for copy in copies:
+        copy.wait()
 
 
 def local(
@@ -492,7 +507,7 @@
     vmem = pl.BlockSpec(memory_space=pltpu.VMEM)
     hbm = pl.BlockSpec(memory_space=pltpu.HBM)
     dma = pltpu.SemaphoreType.DMA
-    return pl.pallas_call(
+    new_spectrum, stress = pl.pallas_call(
         functools.partial(kernel, tiles, sects),
         out_shape=(
             jax.ShapeDtypeStruct(spectrum.shape, F32),
@@ -553,6 +568,18 @@
         ocean_slot.reshape(rows, columns),
         spectrum,
     )
+    return pl.pallas_call(
+        hand_on,
+        out_shape=(
+            jax.ShapeDtypeStruct(new_spectrum.shape, F32),
+            jax.ShapeDtypeStruct(stress.shape, F32),
+        ),
+        in_specs=[hbm, hbm],
+        out_specs=(hbm, hbm),
+        scratch_shapes=[dma((COPIES + 1,))],
+        compiler_params=pltpu.CompilerParams(vmem_limit_bytes=60 * 1024 * 1024),
+        name="hand_on",
+    )(new_spectrum, stress)
 
 
 def solution(mesh):

time: 53.6 us -> 92.8 us (1.73)
  Pallas kernels: 49.7 us -> 92 us
  local copies, waits for them, and re-layouts: 3.09 us -> 0 us
    pallas_call x0 -> x1, Pallas kernels: none -> 42.4 us  [local(): pl.pallas_call(hand_on, out_shape=(jax.ShapeDtypeStruct(new_spectrum.shap...]
    unnamed x4 -> x0, local copies, waits for them, and re-layouts: 3.09 us -> none
where the time goes in v6:
time: 92.8 us; the launch traced here: 92.7 us
  Pallas kernels  92 us (99%)
    pallas_call x1, Pallas kernels, local(): pl.pallas_call(functools.partial(kernel, tiles, sects), out_shape=(jax.Sh...  49.7 us
    pallas_call x1, Pallas kernels, local(): pl.pallas_call(hand_on, out_shape=(jax.ShapeDtypeStruct(new_spectrum.shap...  42.4 us

profile of v6, /device:TPU:0, one launch (start us, length us, event | category | flops | bytes accessed | tf_op | source)
XLA Modules:
  0.0 92.7 jit_solution(3913349054436936803)
XLA Ops:
  0.6 49.7 %coupling.1 = (f32[324,8,128]{2,1,0:T(8,128)}, f32[3,2048]{1,0:T(4,128)}) custom-call(f32[80]{0:T(128)} %constant.2.clone.trig_hbm, f32[36]{0:T(128)} %courant_hbm.1, f32[36]{0:T(128)} %ratio_hbm.1, f32[2,2048]{1,0:T(2,128)} %current_hbm.1, f32[16,128]{1,0:T(8,128)} %bitcast.3, s32[8,128]{1,0:T(8,128)} %mask_hbm.1, s32[8,128]{1,0:T(8,128)} %bitcast.4, ...), custom_call_target="tpu_custom_call" | custom-call | flops 66355200 | bytes 2654208 | tf_op jit(solution)/shard_map/coupling/pallas_call | solution.py:510
  50.3 42.4 %hand_on.1 = (f32[324,8,128]{2,1,0:T(8,128)}, f32[3,2048]{1,0:T(4,128)}) custom-call(f32[324,8,128]{2,1,0:T(8,128)} %get-tuple-element.4.spectrum_ref, f32[3,2048]{1,0:T(4,128)} %get-tuple-element.5.stress_ref), custom_call_target="tpu_custom_call" | custom-call | tf_op jit(solution)/shard_map/hand_on/pallas_call | solution.py:571

commit v7 on v6

--- a/solution.py
+++ b/solution.py
@@ -479,18 +479,22 @@
         cell_copy(k, tile).wait_send()
 
 
-def hand_on(spectrum_ref, stress_ref, spectrum_out, stress_out, sems):
+def hand_on(spectrum_ref, stress_ref, spectrum_out, stress_out, held, held_stress, into, out_of):
     bins = spectrum_ref.shape[0]
-    copies = [pltpu.make_async_copy(stress_ref, stress_out, sems.at[COPIES])]
+    loads = [pltpu.make_async_copy(stress_ref, held_stress, into.at[COPIES])]
+    stores = [pltpu.make_async_copy(held_stress, stress_out, out_of.at[COPIES])]
     for i in range(COPIES):
-        at = pl.ds(bins * i // COPIES, bins * (i + 1) // COPIES - bins * i // COPIES)
-        copies.append(
-            pltpu.make_async_copy(spectrum_ref.at[at], spectrum_out.at[at], sems.at[i])
-        )
-    for copy in copies:
-        copy.start()
-    for copy in copies:
-        copy.wait()
+        begin, end = bins * i // COPIES, bins * (i + 1) // COPIES
+        at = pl.ds(begin, end - begin)
+        loads.append(pltpu.make_async_copy(spectrum_ref.at[at], held.at[at], into.at[i]))
+        stores.append(pltpu.make_async_copy(held.at[at], spectrum_out.at[at], out_of.at[i]))
+    for load in loads:
+        load.start()
+    for load, store in zip(loads, stores):
+        load.wait()
+        store.start()
+    for store in stores:
+        store.wait()
 
 
 def local(
@@ -576,7 +580,12 @@
         ),
         in_specs=[hbm, hbm],
         out_specs=(hbm, hbm),
-        scratch_shapes=[dma((COPIES + 1,))],
+        scratch_shapes=[
+            pltpu.VMEM(new_spectrum.shape, F32),
+            pltpu.VMEM(stress.shape, F32),
+            dma((COPIES + 1,)),
+            dma((COPIES + 1,)),
+        ],
         compiler_params=pltpu.CompilerParams(vmem_limit_bytes=60 * 1024 * 1024),
         name="hand_on",
     )(new_spectrum, stress)

time: 92.8 us -> 52.7 us (0.57)
  Pallas kernels: 92 us -> 51.9 us
    pallas_call x1, Pallas kernels: 42.4 us -> 2.23 us  [local(): pl.pallas_call(hand_on, out_shape=(jax.ShapeDtypeStruct(new_spectrum.shap...]
where the time goes in v7:
time: 52.7 us; the launch traced here: 52.5 us
  Pallas kernels  51.9 us (98%)
  between operations  0.64 us (1%)
    pallas_call x1, Pallas kernels, local(): pl.pallas_call(functools.partial(kernel, tiles, sects), out_shape=(jax.Sh...  49.7 us
    pallas_call x1, Pallas kernels, local(): pl.pallas_call(hand_on, out_shape=(jax.ShapeDtypeStruct(new_spectrum.shap...  2.23 us

profile of v7, /device:TPU:0, one launch (start us, length us, event | category | flops | bytes accessed | tf_op | source)
XLA Modules:
  0.0 52.5 jit_solution(15482637890409160712)
XLA Ops:
  0.6 49.7 %coupling.1 = (f32[324,8,128]{2,1,0:T(8,128)}, f32[3,2048]{1,0:T(4,128)}) custom-call(f32[80]{0:T(128)} %constant.2.clone.trig_hbm, f32[36]{0:T(128)} %courant_hbm.1, f32[36]{0:T(128)} %ratio_hbm.1, f32[2,2048]{1,0:T(2,128)} %current_hbm.1, f32[16,128]{1,0:T(8,128)} %bitcast.3, s32[8,128]{1,0:T(8,128)} %mask_hbm.1, s32[8,128]{1,0:T(8,128)} %bitcast.4, ...), custom_call_target="tpu_custom_call" | custom-call | flops 66355200 | bytes 2654208 | tf_op jit(solution)/shard_map/coupling/pallas_call | solution.py:514
  50.3 2.2 %hand_on.1 = (f32[324,8,128]{2,1,0:T(8,128)}, f32[3,2048]{1,0:T(4,128)}) custom-call(f32[324,8,128]{2,1,0:T(8,128)} %get-tuple-element.4.spectrum_ref, f32[3,2048]{1,0:T(4,128)} %get-tuple-element.5.stress_ref), custom_call_target="tpu_custom_call" | custom-call | tf_op jit(solution)/shard_map/hand_on/pallas_call | solution.py:575
